TPU v7x, 256 devices: a whole 4x4x8 slice. The times are simulated.
256 devices in a mesh: seq: 32 (over y, z), head: 8 (over x, core).
Axes of the slice: x: 4, y: 4, z: 8, core: 2. Of those that a mesh axis runs over, the one named last changes fastest.
Arguments:
- queries: bfloat16 [32768, 2048], P('seq', 'head'), may hold values from -6 to 6
- keys: bfloat16 [32768, 2048], P('seq', 'head'), may hold values from -6 to 6
- values: bfloat16 [32768, 4096], P('seq', 'head'), may hold values from -6 to 6
- input_gate: float32 [8, 32768], P('head', 'seq'), may hold values from -6 to 86
- forget_gate: float32 [8, 32768], P('head', 'seq'), may hold values from 0 to 20
- doc_start: int32 [32768], P('seq'), may hold values from 0 to 1, as said below
- carry_memory: float32 [8, 256, 512], P('head'), may hold values from -24 to 24
- carry_norm: float32 [8, 256], P('head'), may hold values from -24 to 24
- carry_max: float32 [8], P('head'), may hold values from 2 to 86
- out_weight: bfloat16 [4096, 4096], P('seq', 'head'), may hold values from -0.09375 to 0.09375
Outputs:
- mixed: bfloat16 [32768, 4096], P('seq', 'head')
Inputs may be any that keep to these rules, and one draw needn't show every extreme that they name: `doc_start`: exactly one token of the window begins a document, never the first.
All inputs are finite; a program needn't handle non-finite values.
Results may differ from a plain program's by a relative error of at most 0.019.
Values may be sent and summed in bfloat16 or wider, within the bound.
A program may use at most 128 MiB of HBM per device.

v0:
```python
import jax
import jax.numpy as jnp
from jax import lax
from jax.sharding import PartitionSpec as P

DK = 256
DV = 512


HIGH = lax.Precision.HIGHEST


def entering(part, axis, combine, identity):
    place = lax.axis_index(axis)
    gathered = jax.tree.map(lambda a: lax.all_gather(a, axis), part)
    state = jax.tree.map(lambda a, e: jnp.zeros_like(a) + jnp.asarray(e, a.dtype), part, identity)

    def one(hop, state):
        return combine(
            state, jax.tree.map(lambda a: lax.dynamic_index_in_dim(a, hop, 0, False), gathered)
        )

    return lax.fori_loop(0, place, one, state)


def block_terms(queries, keys, values, input_gate, forget_gate, starts):
    steps = queries.shape[0]
    heads = queries.shape[1] // DK
    scale = DK ** (-0.5)
    q_three = queries.reshape(steps, heads, DK)
    k_three = keys.reshape(steps, heads, DK)
    v_three = values.reshape(steps, heads, DV)
    decay = jnp.cumsum(jax.nn.log_sigmoid(forget_gate), axis=1)
    segment = jnp.cumsum(starts)
    places = jnp.arange(steps)
    allowed = (places[None, :] <= places[:, None]) & (segment[None, :] == segment[:, None])
    expo = decay[:, :, None] - decay[:, None, :] + input_gate[:, None, :]
    expo = jnp.where(allowed[None], expo, -1e30)
    local_max = jnp.max(expo, axis=2)
    scores = (
        jnp.einsum("thd,shd->hts", q_three, k_three, preferred_element_type=jnp.float32) * scale
    )
    weights = jnp.exp(expo - local_max[:, :, None]) * scores
    local_den = jnp.sum(weights, axis=2)
    local_num = jnp.einsum(
        "hts,shv->htv", weights.astype(jnp.bfloat16), v_three, preferred_element_type=jnp.float32
    )
    coeff = jnp.exp(expo[:, -1, :] - local_max[:, -1:])
    keyed = k_three.astype(jnp.float32) * jnp.transpose(coeff)[:, :, None] * scale
    block_normalizer_sum = jnp.sum(keyed, axis=0)
    block_memory = jnp.einsum(
        "shd,shv->hdv", keyed.astype(jnp.bfloat16), v_three, preferred_element_type=jnp.float32
    )
    reset = jnp.broadcast_to((segment[-1] > 0).astype(jnp.float32), (heads,))
    summary = (block_memory, block_normalizer_sum, local_max[:, -1], decay[:, -1], reset)
    return (local_num, local_den, local_max, decay, segment, summary)


def combine(earlier, later):
    keep = later[4] < 0.5
    inward = earlier[2] + later[3]
    top = jnp.where(keep, jnp.maximum(inward, later[2]), later[2])
    first = jnp.where(keep, jnp.exp(jnp.minimum(inward - top, 0.0)), 0.0)
    second = jnp.exp(later[2] - top)
    memory = first[:, None, None] * earlier[0] + second[:, None, None] * later[0]
    normal = first[:, None] * earlier[1] + second[:, None] * later[1]
    return (memory, normal, top, earlier[3] + later[3], jnp.maximum(earlier[4], later[4]))


def finish(queries, local_num, local_den, local_max, decay, segment, entry):
    steps = queries.shape[0]
    heads = queries.shape[1] // DK
    q_three = queries.reshape(steps, heads, DK).astype(jnp.float32)
    fresh = (segment == 0)[None, :]
    inward = entry[2][:, None] + decay
    merged = jnp.where(fresh, jnp.maximum(inward, local_max), local_max)
    carried = jnp.where(fresh, jnp.exp(jnp.minimum(inward - merged, 0.0)), 0.0)
    own = jnp.exp(local_max - merged)
    state_numerator = jnp.einsum("thd,hdv->htv", q_three, entry[0], precision=HIGH)
    state_den = jnp.einsum("thd,hd->ht", q_three, entry[1], precision=HIGH)
    numer = own[:, :, None] * local_num + carried[:, :, None] * state_numerator
    denom = own * local_den + carried * state_den
    hidden = numer / jnp.maximum(jnp.abs(denom), 1.0)[:, :, None]
    return jnp.transpose(hidden, (1, 0, 2)).reshape(steps, heads * DV).astype(jnp.bfloat16)


def shards(
    queries,
    keys,
    values,
    input_gate,
    forget_gate,
    doc_start,
    carry_memory,
    carry_norm,
    carry_max,
    out_weight,
):
    heads = queries.shape[1] // DK
    local_num, local_den, local_max, decay, segment, summary = block_terms(
        queries, keys, values, input_gate, forget_gate, doc_start
    )
    blank = (
        jnp.zeros((heads, DK, DV), jnp.float32),
        jnp.zeros((heads, DK), jnp.float32),
        jnp.full((heads,), -1e30, jnp.float32),
        jnp.zeros((heads,), jnp.float32),
        jnp.zeros((heads,), jnp.float32),
    )
    prefix = entering(
        (summary[0], summary[1], summary[2], summary[3], summary[4]), "seq", combine, blank
    )
    seed = (
        carry_memory,
        carry_norm,
        carry_max,
        jnp.zeros((heads,), jnp.float32),
        jnp.ones((heads,), jnp.float32),
    )
    entry = combine(seed, prefix)
    hidden = finish(queries, local_num, local_den, local_max, decay, segment, entry)
    full_rows = lax.all_gather(out_weight, "seq", axis=0, tiled=True)
    own_rows = lax.all_to_all(full_rows, "head", split_axis=0, concat_axis=1, tiled=True)
    partial_value = jnp.dot(hidden, own_rows, preferred_element_type=jnp.float32)
    mixed = lax.psum_scatter(
        partial_value.astype(jnp.bfloat16), "head", scatter_dimension=1, tiled=True
    )
    return mixed


def solution(mesh):
    placed = (
        P("seq", "head"),
        P("seq", "head"),
        P("seq", "head"),
        P("head", "seq"),
        P("head", "seq"),
        P("seq"),
        P("head", None, None),
        P("head", None),
        P("head"),
        P("seq", "head"),
    )
    return jax.shard_map(
        shards, mesh=mesh, in_specs=placed, out_specs=P("seq", "head"), check_vma=False
    )
```

profile of v0, /device:TPU:1, one launch (start us, length us, event | category | flops | bytes accessed | tf_op | source)
XLA Modules:
  0.0 521.1 jit_solution(4405988119777743983)
XLA Ops:
  6.5 0.0 copy-start
  6.5 0.0 all-gather.7.cloned.1.call-start
  6.5 0.7 all-gather.7.cloned.1.call-update
  7.3 0.0 all-gather.9.cloned.1.call-start
  7.3 1.0 reduce-window.15
  8.3 0.1 slice.26
  8.4 0.7 fusion.28
  9.1 0.3 reduce-window.19
  9.4 0.2 slice_reduce_fusion.1
  9.6 0.2 reduce-window.24
  9.7 0.1 slice_reduce_fusion
  9.9 0.1 bitcast_add_fusion.2
  9.9 0.1 broadcast_compare_fusion
  10.0 1.7 add_select_fusion
  11.7 0.6 slice.37
  12.3 0.6 fusion.29
  13.0 0.0 copy-done
  13.0 1.6 fusion.12
  14.6 0.0 all-gather.9.cloned.1.call-update
  14.6 78.3 %all-gather.7.cloned.1.call-done = bf16[4096,512]{1,0:T(8,128)(2,1)} async-done(((bf16[128,512]{1,0:T(8,128)(2,1)}), bf16[4096,512]{1,0:T(8,128)(2,1)}) %all-gather.7.cloned.1.call-update) | async-done | bytes 4194320 | tf_op jit(solution)/shard_map/all_gather | solution.py:122
  92.9 7.9 %all-to-all-start = ((bf16[8,512,512]{2,1,0:T(8,128)(2,1)}), bf16[8,512,512]{2,1,0:T(8,128)(2,1)}, u32[]{:S(2)}, u32[]{:S(2)}) async-start(bf16[8,512,512]{2,1,0:T(8,128)(2,1)} %bitcast.85), calls=%async_computation | async-start | bytes 8388608 | tf_op jit(solution)/shard_map/all_to_all | solution.py:123
  100.8 0.1 broadcast.221
  100.9 0.6 slice.36
  101.5 0.6 slice.35
  102.7 0.0 copy-done.7
  102.7 0.6 dynamic-slice
  103.3 1.2 bitcast_dynamic-update-slice_fusion
  105.8 0.6 bitcast_dynamic-update-slice_fusion.1
  106.4 0.7 fusion.35
  107.1 59.2 %all-reduce.3 = (f32[32]{0:T(128)S(1)}, f32[32]{0:T(128)S(1)}, f32[32]{0:T(128)S(1)}) all-reduce(f32[32]{0:T(128)S(1)} %fusion.35, f32[32]{0:T(128)S(1)} %bitcast_dynamic-update-slice_fusion.1, f32[32]{0:T(128)S(1)} %bitcast_dynamic-update-slice_fusion), channel_id=2, replica_groups=mesh['seq'=32,'head'=8] {'seq'}, use_global_device_ids=true, to_apply=%add | all-reduce | flops 96 | bytes 768
  166.3 0.2 fusion.10
  166.5 35.0 %all-gather.3 = f32[32,1,256]{2,1,0:T(1,128)S(1)} all-gather(f32[1,1,256]{2,1,0:T(1,128)S(1)} %bitcast.95), channel_id=4, replica_groups=mesh['seq'=32,'head'=8] {'seq'}, dimensions={0}, use_global_device_ids=true | all-gather | bytes 33792 | tf_op jit(solution)/shard_map/all_gather | solution.py:15
  201.5 0.0 copy-done.4
  201.5 2.4 fusion.41
  204.0 2.7 fusion.7
  206.7 0.0 all-to-all-done
  206.7 6.5 %copy.21 = bf16[512,8,512]{0,2,1:T(8,128)(2,1)} copy(bf16[512,8,512]{2,0,1:T(8,128)(2,1)} %bitcast.37) | data formatting | bytes 8388608 | tf_op jit(solution)/shard_map/all_to_all | solution.py:123
  213.1 23.2 %all-gather.9.cloned.1.call-done = f32[8192,512]{1,0:T(8,128)} async-done(((f32[256,512]{1,0:T(8,128)}), f32[8192,512]{1,0:T(8,128)}) %all-gather.9.cloned.1.call-update) | async-done | bytes 16777232 | tf_op jit(solution)/shard_map/all_gather | solution.py:15
  236.4 0.0 copy-start.5
  236.5 0.0 copy-start.6
  236.6 0.5 copy-done.5
  237.1 0.5 fusion.30
  237.7 0.0 copy-done.6
  237.7 0.0 copy-start.1
  237.7 3.1 fusion.6
  240.8 6.7 %convolution_convert_fusion = bf16[1024,4096]{1,0:T(8,128)(2,1)} fusion(bf16[1024,512]{1,0:T(8,128)(2,1)S(1)} %fusion.6, bf16[512,4096]{0,1:T(8,128)(2,1)S(1)} %bitcast.84), kind=kOutput, calls=%fused_computation.8 | convolution fusion | flops 4299161600 | bytes 13631488 | tf_op jit(solution)/shard_map/dot_general | solution.py:124
  247.5 0.0 reduce-scatter.2.cloned.1.call-update
  247.5 267.0 %reduce-scatter.2.cloned.1.call-done = bf16[1024,512]{1,0:T(8,128)(2,1)} async-done(((bf16[1024,4096]{1,0:T(8,128)(2,1)}), bf16[1024,512]{1,0:T(8,128)(2,1)}) %reduce-scatter.2.cloned.1.call-update) | async-done | bytes 1048592 | tf_op jit(solution)/shard_map/reduce_scatter | solution.py:125
  (17 shorter events, 0.1 us)
Async XLA Ops:
  6.5 6.5 %copy-start = (bf16[1024,512]{1,0:T(8,128)(2,1)S(1)}, bf16[1024,512]{1,0:T(8,128)(2,1)}, u32[]{:S(2)}) copy-start(bf16[1024,512]{1,0:T(8,128)(2,1)} %param.14) | copy-start | bytes 3145732
  6.5 6.5 %copy-start.2 = (bf16[1024,256]{1,0:T(8,128)(2,1)S(1)}, bf16[1024,256]{1,0:T(8,128)(2,1)}, u32[]{:S(2)}) copy-start(bf16[1024,256]{1,0:T(8,128)(2,1)} %param.13) | copy-start | bytes 1572868
  6.5 86.4 %all-gather.7.cloned.1.call-start = ((), (), s32[]{:S(2)}) async-start(), calls=%async_computation.2 | async-start | bytes 4325376 | tf_op jit(solution)/shard_map/all_gather | solution.py:122
  7.3 229.1 %all-gather.9.cloned.1.call-start = ((), (), s32[]{:S(2)}) async-start(), calls=%async_computation.4 | async-start | bytes 17301504 | tf_op jit(solution)/shard_map/all_gather | solution.py:15
  92.9 9.8 %copy-start.7 = (u32[256]{0:T(256)S(1)}, u32[256]{0:T(256)}, u32[]{:S(2)}) copy-start(u32[256]{0:T(256)} %constant.74) | copy-start | bytes 3076
  92.9 108.6 %copy-start.3 = (bf16[1024,256]{1,0:T(8,128)(2,1)S(1)}, bf16[1024,256]{1,0:T(8,128)(2,1)}, u32[]{:S(2)}) copy-start(bf16[1024,256]{1,0:T(8,128)(2,1)} %param.12) | copy-start | bytes 1572868
  92.9 108.6 %copy-start.4 = (f32[1,1024]{1,0:T(1,128)S(1)}, f32[1,1024]{1,0:T(1,128)}, u32[]{:S(2)}) copy-start(f32[1,1024]{1,0:T(1,128)} %param.15) | copy-start | bytes 12292
  92.9 113.7 %all-to-all-start = ((bf16[8,512,512]{2,1,0:T(8,128)(2,1)}), bf16[8,512,512]{2,1,0:T(8,128)(2,1)}, u32[]{:S(2)}, u32[]{:S(2)}) async-start(bf16[8,512,512]{2,1,0:T(8,128)(2,1)} %bitcast.85), calls=%async_computation | async-start | bytes 8388608 | tf_op jit(solution)/shard_map/all_to_all | solution.py:123
  100.8 413.7 %reduce-scatter.2.cloned.1.call-start = ((), (), s32[]{:S(2)}) async-start(), calls=%async_computation.3 | async-start | bytes 9437184 | tf_op jit(solution)/shard_map/reduce_scatter | solution.py:125
  236.4 0.7 copy-start.5
  236.5 1.2 copy-start.6
  237.7 3.1 copy-start.1
Sparse Core Ops, SparseCore 0:
  10.0 82.9 all-gather.6
  95.5 140.7 all-gather.8
  247.7 266.8 reduce-scatter.1
where the time goes:
time: 525 us; the launch traced here: 521 us
  waiting for transfers between devices  369 us (70%)
  blocking collectives  94.2 us (18%)
  matrix products  17 us (3%)
  between operations  15.2 us (3%)
  local copies, waits for them, and re-layouts  11.7 us (2%)
  starting transfers between devices  7.91 us (2%)
  other arithmetic  5.66 us (1%)
    reduce_scatter x1, waiting for transfers between devices, shards(): lax.psum_scatter(partial_value.astype(jnp.bfloat16), 'head', scatter_dime...  267 us
    all_gather x1, waiting for transfers between devices, shards(): full_rows = lax.all_gather(out_weight, 'seq', axis=0, tiled=True)  78.3 us
    unnamed x1, blocking collectives  59.2 us
    all_gather x1, blocking collectives, entering(): gathered = jax.tree.map(lambda a: lax.all_gather(a, axis), part)  35 us
    all_gather x1, waiting for transfers between devices, entering(): gathered = jax.tree.map(lambda a: lax.all_gather(a, axis), part)  23.2 us
  transfers between devices with their start and end apart: 4, of which 3 were waited for; matrix products, arithmetic and copies ran while one was open for 5% of the time, Pallas kernels for 0%

commit v1 on v0

v1 whole, which is shorter than its diff:
```python
import jax
import jax.numpy as jnp
from jax import lax
from jax.experimental import pallas as pl
from jax.experimental.pallas import tpu as pltpu
from jax.sharding import PartitionSpec as P

DK = 256
DV = 512
TOK = 1024
NY, NZ = 4, 8
NS = NY * NZ
LOW = -1e30
MESH = pl.DeviceIdType.MESH
F32, BF16 = jnp.float32, jnp.bfloat16
QT = 256
XT = 128
NXT = TOK // XT


def lane_scan(a, op, fill, seg=None):
    lane = lax.broadcasted_iota(jnp.int32, a.shape, 1)
    for sh in (1, 2, 4, 8, 16, 32, 64):
        ok = lane >= sh
        if seg is not None:
            ok = ok & (pltpu.roll(seg, sh, 1) == seg)
        a = op(a, jnp.where(ok, pltpu.roll(a, sh, 1), fill))
    return a


def row_scan(a, op, fill, seg=None):
    row = lax.broadcasted_iota(jnp.int32, a.shape, 0)
    for sh in (1, 2, 4):
        ok = row >= sh
        if seg is not None:
            ok = ok & (pltpu.roll(seg, sh, 0) == seg)
        a = op(a, jnp.where(ok, pltpu.roll(a, sh, 0), fill))
    return a


def last_lane(a):
    return jnp.broadcast_to(a[:, 127:128], a.shape)


def before(a, fill):
    row = lax.broadcasted_iota(jnp.int32, a.shape, 0)
    return jnp.where(row >= 1, pltpu.roll(a, 1, 0), fill)


def running_sum(a):
    inside = lane_scan(a, jnp.add, 0.0)
    return inside + before(row_scan(last_lane(inside), jnp.add, 0.0), 0.0)


def running_max(a, seg):
    inside = lane_scan(a, jnp.maximum, LOW, seg)
    seg_end = last_lane(seg)
    ends = row_scan(last_lane(inside), jnp.maximum, LOW, seg_end)
    carried = jnp.where(before(seg_end, -1.0) == seg, before(ends, LOW), LOW)
    return jnp.maximum(inside, carried)


def column(cols, tile, size):
    per = size // 128
    return jnp.concatenate([cols[:, tile * per + i : tile * per + i + 1] for i in range(per)], 0)


def as_row(a, rows):
    return jnp.concatenate([a[i : i + 1, :] for i in range(rows)], 1)


def kernel(
    q_ref, k_ref, v_ref, ig_ref, fg_ref, ds_ref, cmem_ref, cnorm_ref, cmax_ref, w_ref,
    out_ref,
    wbuf, stats, cpack, crecv, epack, erecv, num, den, hid, part_out, part_in, acc, gates,
    wsend, wrecv, swap_send, ssend, srecv, csend, crecv_sem, esend, erecv_sem,
    hsend, hrecv, psend, precv,
):
    me = lax.axis_index("seq")
    head = lax.axis_index("head")
    y, z = me // NZ, me % NZ
    x, core = head // 2, head % 2
    mate = 1 - core
    near = (x // 2) * 2 + (1 - x % 2)
    far = 3 - x
    home = (y // 2) == (x // 2)
    swap_seq = ((y + 2) % NY) * NZ + z

    def at(yy, zz):
        return ((yy + NY) % NY) * NZ + (zz + NZ) % NZ

    barrier = pltpu.get_barrier_semaphore()

    def greet(seq, hd):
        pl.semaphore_signal(
            barrier, inc=1, device_id={"seq": seq, "head": hd}, device_id_type=MESH
        )

    def greet_seq(d, c):
        greet((me + d) % NS, head)
        return c

    lax.fori_loop(1, NS, greet_seq, 0)
    greet(me, x * 2 + mate)
    greet(me, near * 2 + core)
    greet(me, far * 2 + core)

    @pl.when(jnp.logical_not(home))
    def _():
        greet(swap_seq, far * 2 + core)

    def w_copy(slot, dev):
        return pltpu.make_async_remote_copy(
            src_ref=wbuf.at[slot], dst_ref=wbuf.at[slot], send_sem=wsend,
            recv_sem=wrecv.at[slot], device_id={"seq": dev, "head": head},
            device_id_type=MESH,
        )

    def swap_copy():
        return pltpu.make_async_remote_copy(
            src_ref=w_ref, dst_ref=wbuf.at[swap_seq], send_sem=swap_send,
            recv_sem=wrecv.at[swap_seq], device_id={"seq": swap_seq, "head": far * 2 + core},
            device_id_type=MESH,
        )

    def w_sends(slot, zs, ys):
        for dz in zs:
            w_copy(slot, at(y, z + dz)).start()
        for dy in ys:
            w_copy(slot, at(y + dy, z)).start()

    def w_wait(slot):
        w_copy(slot, me).wait_recv()

    lf = fg_ref[...]
    lf = jnp.minimum(lf, 0.0) - jnp.log1p(jnp.exp(-jnp.abs(lf)))
    decay = running_sum(lf)
    seg = running_sum(ds_ref[...].astype(F32))
    u = ig_ref[...] - decay
    top = running_max(u, seg)
    local_max = decay + top
    end = lambda a: jnp.broadcast_to(a[7:8, 127:128], (1, 128))
    seg_end = end(seg)
    coeff = jnp.where(seg == seg_end, jnp.exp(jnp.minimum(u - end(top), 0.0)), 0.0) * (DK**-0.5)
    coeff_cols = jnp.transpose(coeff)
    top_cols = jnp.transpose(top)
    seg_cols = jnp.transpose(seg)
    keyed = [
        k_ref[i * 128 : (i + 1) * 128, :].astype(F32) * coeff_cols[:, i : i + 1] for i in range(8)
    ]
    normal = sum(jnp.sum(t, axis=0, keepdims=True) for t in keyed)
    stats[me, 0:1, :] = normal[:, :128]
    stats[me, 1:2, :] = normal[:, 128:]
    stats[me, 2:3, :] = end(local_max)
    stats[me, 3:4, :] = end(decay)
    stats[me, 4:5, :] = jnp.where(seg_end > 0.5, 1.0, 0.0)

    waits = jnp.where(home, 34, 35)
    pl.semaphore_wait(barrier, waits)

    @pl.when(home)
    def _():
        wbuf[me] = w_ref[...]
        w_sends(me, (1, -1), (1, -1))

    @pl.when(jnp.logical_not(home))
    def _():
        swap_copy().start()

    def stats_copy(dev):
        return pltpu.make_async_remote_copy(
            src_ref=stats.at[me], dst_ref=stats.at[me], send_sem=ssend, recv_sem=srecv,
            device_id={"seq": dev, "head": head}, device_id_type=MESH,
        )

    def send_stats(d, c):
        stats_copy((me + d) % NS).start()
        return c

    lax.fori_loop(1, NS, send_stats, 0)

    memory = lax.dot_general(
        jnp.concatenate([t.astype(BF16) for t in keyed], 0), v_ref[...],
        (((0,), (0,)), ((), ())), preferred_element_type=F32,
    ).astype(BF16)
    cpack[0:16] = memory[:, :256].reshape(16, 16, 256)
    cpack[16:32] = memory[:, 256:].reshape(16, 16, 256)
    crecv[me] = cpack[me]

    def c_copy(dev):
        return pltpu.make_async_remote_copy(
            src_ref=cpack.at[dev], dst_ref=crecv.at[me], send_sem=csend, recv_sem=crecv_sem,
            device_id={"seq": dev, "head": head}, device_id_type=MESH,
        )

    def send_c(d, c):
        c_copy((me + d) % NS).start()
        return c

    lax.fori_loop(1, NS, send_c, 0)

    @pl.when(jnp.logical_not(home))
    def _():
        swap_copy().wait_send()
        w_wait(me)
        w_sends(me, (1, -1), (1, -1))

    def attend(tile):
        n = (tile + 1) * QT
        qt = q_ref[tile * QT : (tile + 1) * QT, :]
        scores = lax.dot_general(
            qt, k_ref[:n, :], (((1,), (1,)), ((), ())), preferred_element_type=F32
        )
        blocks = n // 128
        u_row, seg_row = as_row(u, blocks), as_row(seg, blocks)
        place = lax.broadcasted_iota(jnp.int32, (QT, n), 0) + tile * QT
        allowed = (lax.broadcasted_iota(jnp.int32, (QT, n), 1) <= place) & (
            seg_row == column(seg_cols, tile, QT)
        )
        gain = jnp.exp(u_row - column(top_cols, tile, QT))
        weights = jnp.where(allowed, gain * (DK**-0.5), 0.0) * scores
        den[tile * QT : (tile + 1) * QT, :] = jnp.sum(weights, axis=1, keepdims=True)
        num[tile * QT : (tile + 1) * QT, :] = jnp.dot(
            weights.astype(BF16), v_ref[:n, :], preferred_element_type=F32
        )

    def z_step(k):
        w_wait(at(y, z - k))
        w_sends(at(y, z - k), (1,) if k <= 3 else (), (1, -1))
        if k <= 3:
            w_wait(at(y, z + k))
            w_sends(at(y, z + k), (-1,) if k <= 2 else (), (1, -1))

    def y_step(o, up):
        w_wait(at(y - 1, z + o))
        w_wait(at(y + 1, z + o))
        if up:
            w_sends(at(y - 1, z + o), (), (1,))
        else:
            w_sends(at(y + 1, z + o), (), (-1,))

    attend(0)
    z_step(1)
    attend(1)
    attend(2)
    z_step(2)
    attend(3)

    def all_pieces(ref, sem):
        part = ref.at[pl.ds(0, NS - 1)]
        return pltpu.make_async_copy(part, part, sem)

    all_pieces(stats, srecv).wait()
    m = jnp.broadcast_to(cmax_ref[...], (1, 128))
    n0, n1 = cnorm_ref[0:1, :], cnorm_ref[1:2, :]
    em, e0, e1 = m, n0, n1
    firsts, seconds = [], []
    for j in range(NS - 1):
        keep = stats[j, 4:5, :] < 0.5
        inward = m + stats[j, 3:4, :]
        later = stats[j, 2:3, :]
        m = jnp.where(keep, jnp.maximum(inward, later), later)
        first = jnp.where(keep, jnp.exp(jnp.minimum(inward - m, 0.0)), 0.0)
        second = jnp.exp(later - m)
        n0 = first * n0 + second * stats[j, 0:1, :]
        n1 = first * n1 + second * stats[j, 1:2, :]
        here = me == j + 1
        em, e0, e1 = (jnp.where(here, b, a) for a, b in ((em, m), (e0, n0), (e1, n1)))
        gates[j, 0:1, :] = first
        gates[j, 1:2, :] = second

    group, half = me % 16, me // 16
    carry_rows = cmem_ref[pl.ds(pl.multiple_of(group * 16, 16), 16), :]
    state = jnp.where(half == 0, carry_rows[:, :256], carry_rows[:, 256:])
    all_pieces(crecv, crecv_sem).wait()
    epack[0] = state.astype(BF16)
    for j in range(NS - 1):
        first = jnp.concatenate([gates[j, 0:1, :]] * 2, 1)
        second = jnp.concatenate([gates[j, 1:2, :]] * 2, 1)
        state = first * state + second * crecv[j].astype(F32)
        epack[j + 1] = state.astype(BF16)
    erecv[me] = epack[me]

    def e_copy(dev):
        return pltpu.make_async_remote_copy(
            src_ref=epack.at[dev], dst_ref=erecv.at[me], send_sem=esend, recv_sem=erecv_sem,
            device_id={"seq": dev, "head": head}, device_id_type=MESH,
        )

    def send_e(d, c):
        e_copy((me + d) % NS).start()
        return c

    lax.fori_loop(1, NS, send_e, 0)
    z_step(3)

    inward = jnp.broadcast_to(em, (8, 128)) + decay
    fresh = seg < 0.5
    merged = jnp.where(fresh, jnp.maximum(inward, local_max), local_max)
    carried = jnp.where(fresh, jnp.exp(jnp.minimum(inward - merged, 0.0)), 0.0)
    own = jnp.exp(local_max - merged)
    carried_cols, own_cols = jnp.transpose(carried), jnp.transpose(own)
    en = jnp.concatenate([e0, e1], 1)
    high = en.astype(BF16)
    rest = en - high.astype(F32)
    mid = rest.astype(BF16)
    low = (rest - mid.astype(F32)).astype(BF16)
    norms = jnp.concatenate(
        [high.astype(F32), mid.astype(F32), low.astype(F32), jnp.zeros((5, DK), F32)], 0
    ).astype(BF16)
    sden = lax.dot_general(
        q_ref[...], norms, (((1,), (1,)), ((), ())), preferred_element_type=F32
    )
    sden = jnp.sum(sden, axis=1, keepdims=True)
    for i in range(8):
        rows = slice(i * 128, (i + 1) * 128)
        o, c = own_cols[:, i : i + 1], carried_cols[:, i : i + 1]
        whole = o * den[rows, :] + c * sden[rows, :]
        inverse = 1.0 / jnp.maximum(jnp.abs(whole), 1.0)
        den[rows, :] = c * inverse
        num[rows, :] = num[rows, :] * (o * inverse)

    z_step(4)
    all_pieces(erecv, erecv_sem).wait()
    entry_a = erecv[0:16].reshape(256, 256)
    entry_b = erecv[16:32].reshape(256, 256)
    mine, theirs = (x % 2) * 2 + core, (x % 2) * 2 + mate
    other, other_mate = (1 - x % 2) * 2 + core, (1 - x % 2) * 2 + mate

    def rows_of(t):
        return pl.ds(pl.multiple_of(t * XT, XT), XT)

    def h_copy(slot, t, hd):
        return pltpu.make_async_remote_copy(
            src_ref=hid.at[slot, rows_of(t)], dst_ref=hid.at[slot, rows_of(t)], send_sem=hsend,
            recv_sem=hrecv.at[slot, t], device_id={"seq": me, "head": hd}, device_id_type=MESH,
        )

    def make_hidden(t, c):
        rows = rows_of(t)
        qt = q_ref[rows, :]
        scale = den[rows, :]
        for part, e in ((slice(0, 256), entry_a), (slice(256, 512), entry_b)):
            got = jnp.dot(qt, e, preferred_element_type=F32)
            hid[mine, rows, part] = (num[rows, part] + scale * got).astype(BF16)
        h_copy(mine, t, near * 2 + core).start()
        h_copy(mine, t, x * 2 + mate).start()
        return c

    lax.fori_loop(0, NXT, make_hidden, 0)

    order = ((0, True), (-1, True), (1, False), (-2, False), (2, True), (-3, True), (3, False), (-4, False))
    for o, up in order:
        y_step(o, up)
    for o, _ in order:
        w_wait(at(y + 2, z + o))

    def p_copy(t):
        return pltpu.make_async_remote_copy(
            src_ref=part_out.at[rows_of(t)], dst_ref=part_in.at[rows_of(t)], send_sem=psend,
            recv_sem=precv.at[t], device_id={"seq": me, "head": far * 2 + core},
            device_id_type=MESH,
        )

    own_base, far_base = 16 * (x // 2), 16 * (1 - x // 2)

    def project(t, base):
        total = None
        for j in range(4):
            w = wbuf[pl.ds(base + 4 * j, 4)].reshape(DV, DV)
            term = jnp.dot(hid[j, rows_of(t), :], w, preferred_element_type=F32)
            total = term if total is None else total + term
        return total

    def cross(t, c):
        h_copy(other, t, head).wait_recv()
        h_copy(other, t, x * 2 + mate).start()
        h_copy(theirs, t, head).wait_recv()
        h_copy(other_mate, t, head).wait_recv()
        part_out[rows_of(t), :] = project(t, far_base).astype(BF16)
        p_copy(t).start()
        acc[rows_of(t), :] = project(t, own_base)
        return c

    lax.fori_loop(0, NXT, cross, 0)

    def finish(t, c):
        p_copy(t).wait_recv()
        rows = rows_of(t)
        out_ref[rows, :] = (acc[rows, :] + part_in[rows, :].astype(F32)).astype(BF16)
        return c

    lax.fori_loop(0, NXT, finish, 0)

    all_pieces(wbuf, wsend).wait()
    all_pieces(stats, ssend).wait()
    all_pieces(cpack, csend).wait()
    all_pieces(epack, esend).wait()
    whole = hid.at[pl.ds(0, 3)]
    pltpu.make_async_copy(whole, whole, hsend).wait()
    pltpu.make_async_copy(part_out, part_out, psend).wait()


def shards(q, k, v, ig, fg, ds, cmem, cnorm, cmax, w):
    dma = pltpu.SemaphoreType.DMA
    vmem = pl.BlockSpec(memory_space=pltpu.VMEM)
    return pl.pallas_call(
        kernel,
        out_shape=jax.ShapeDtypeStruct((TOK, DV), BF16),
        in_specs=[vmem] * 10,
        out_specs=vmem,
        scratch_shapes=[
            pltpu.VMEM((NS, 128, DV), BF16),
            pltpu.VMEM((NS, 8, 128), F32),
            pltpu.VMEM((NS, 16, 256), BF16),
            pltpu.VMEM((NS, 16, 256), BF16),
            pltpu.VMEM((NS, 16, 256), BF16),
            pltpu.VMEM((NS, 16, 256), BF16),
            pltpu.VMEM((TOK, DV), F32),
            pltpu.VMEM((TOK, 1), F32),
            pltpu.VMEM((4, TOK, DV), BF16),
            pltpu.VMEM((TOK, DV), BF16),
            pltpu.VMEM((TOK, DV), BF16),
            pltpu.VMEM((TOK, DV), F32),
            pltpu.VMEM((NS, 8, 128), F32),
            dma, dma((NS,)), dma, dma, dma, dma, dma, dma, dma,
            dma, dma((4, NXT)), dma, dma((NXT,)),
        ],
        compiler_params=pltpu.CompilerParams(
            collective_id=0, has_side_effects=True, vmem_limit_bytes=56 * 2**20
        ),
    )(
        q, k, v, ig.reshape(8, 128), fg.reshape(8, 128), ds.reshape(8, 128),
        cmem.reshape(DK, DV), cnorm.reshape(2, 128), cmax.reshape(1, 1), w,
    )


def solution(mesh):
    placed = (
        P("seq", "head"),
        P("seq", "head"),
        P("seq", "head"),
        P("head", "seq"),
        P("head", "seq"),
        P("seq"),
        P("head", None, None),
        P("head", None),
        P("head"),
        P("seq", "head"),
    )
    return jax.shard_map(
        shards, mesh=mesh, in_specs=placed, out_specs=P("seq", "head"), check_vma=False
    )
```

time: 525 us -> 91.7 us (0.17)
  waiting for transfers between devices: 369 us -> 0 us
  blocking collectives: 94.2 us -> 0 us
  Pallas kernels: 0 us -> 88.6 us
  matrix products: 17 us -> 0 us
  between operations: 15.2 us -> 0.66 us
  local copies, waits for them, and re-layouts: 11.7 us -> 2.26 us
  starting transfers between devices: 7.91 us -> 0 us
  other arithmetic: 5.66 us -> 0 us
    reduce_scatter x1 -> x0, waiting for transfers between devices: 267 us -> none  [shards(): lax.psum_scatter(partial_value.astype(jnp.bfloat16), 'head', scatter_dime...]
    all_gather x2 -> x0, waiting for transfers between devices: 102 us -> none  [the longest x1 78.3 us: shards(): full_rows = lax.all_gather(out_weight, 'seq', axis=0, tiled=True)]
    pallas_call x0 -> x1, Pallas kernels: none -> 88.6 us  [shards(): pl.pallas_call(kernel, out_shape=jax.ShapeDtypeStruct((TOK, DV), BF16), i...]
    unnamed x1 -> x0, blocking collectives: 59.2 us -> none
    all_gather x1 -> x0, blocking collectives: 35 us -> none  [entering(): gathered = jax.tree.map(lambda a: lax.all_gather(a, axis), part)]
    dot_general x6 -> x0, matrix products: 17 us -> none  [the longest x1 6.74 us: shards(): jnp.dot(hidden, own_rows, preferred_element_type=jnp.float32)]
    all_to_all x1 -> x0, starting transfers between devices: 7.87 us -> none  [shards(): lax.all_to_all(full_rows, 'head', split_axis=0, concat_axis=1, tiled=True)]
    all_to_all x1 -> x0, local copies, waits for them, and re-layouts: 6.47 us -> none  [shards(): lax.all_to_all(full_rows, 'head', split_axis=0, concat_axis=1, tiled=True)]
  transfers between devices with their start and end apart: 4 -> 0, of which waited for: 3 -> 0; matrix products, arithmetic and copies ran while one was open for 5% -> 0% of each run, Pallas kernels for 0% -> 0%
where the time goes in v1:
time: 91.7 us; the launch traced here: 91.5 us
  Pallas kernels  88.6 us (97%)
  local copies, waits for them, and re-layouts  2.26 us (2%)
    pallas_call x1, Pallas kernels, shards(): pl.pallas_call(kernel, out_shape=jax.ShapeDtypeStruct((TOK, DV), BF16), i...  88.6 us
    unnamed x1, local copies, waits for them, and re-layouts  2.26 us

profile of v1, /device:TPU:1, one launch (start us, length us, event | category | flops | bytes accessed | tf_op | source)
XLA Modules:
  0.0 91.5 jit_solution(17371584737558364305)
XLA Ops:
  0.7 88.6 %shard_map.100 = bf16[1024,512]{1,0:T(8,128)(2,1)} custom-call(bf16[1024,256]{1,0:T(8,128)(2,1)} %q_ref.1, bf16[1024,256]{1,0:T(8,128)(2,1)} %k_ref.1, bf16[1024,512]{1,0:T(8,128)(2,1)} %v_ref.1, f32[8,128]{1,0:T(8,128)} %bitcast.8, f32[8,128]{1,0:T(8,128)} %bitcast.9, s32[8,128]{1,0:T(8,128)} %bitcast.10, f32[256,512]{1,0:T(8,128)} %bitcast.7, ...), custom_call_target="tpu_custom_call" | custom-call | tf_op jit(solution)/shard_map/pallas_call | solution.py:407
  89.3 2.3 %copy.13 = bf16[1024,512]{1,0:T(8,128)(2,1)} copy(bf16[1024,512]{1,0:T(8,128)(2,1)} %shard_map.100) | data formatting | bytes 2097152

commit v2 on v1

v2 whole, which is shorter than its diff:
```python
import jax
import jax.numpy as jnp
from jax import lax
from jax.experimental import pallas as pl
from jax.experimental.pallas import tpu as pltpu
from jax.sharding import PartitionSpec as P

DK = 256
DV = 512
TOK = 1024
NY, NZ = 4, 8
NS = NY * NZ
LOW = -1e30
MESH = pl.DeviceIdType.MESH
F32, BF16 = jnp.float32, jnp.bfloat16
QT = 256
XT = 128
NXT = TOK // XT


def lane_scan(a, op, fill, seg=None):
    lane = lax.broadcasted_iota(jnp.int32, a.shape, 1)
    for sh in (1, 2, 4, 8, 16, 32, 64):
        ok = lane >= sh
        if seg is not None:
            ok = ok & (pltpu.roll(seg, sh, 1) == seg)
        a = op(a, jnp.where(ok, pltpu.roll(a, sh, 1), fill))
    return a


def row_scan(a, op, fill, seg=None):
    row = lax.broadcasted_iota(jnp.int32, a.shape, 0)
    for sh in (1, 2, 4):
        ok = row >= sh
        if seg is not None:
            ok = ok & (pltpu.roll(seg, sh, 0) == seg)
        a = op(a, jnp.where(ok, pltpu.roll(a, sh, 0), fill))
    return a


def last_lane(a):
    return jnp.broadcast_to(a[:, 127:128], a.shape)


def before(a, fill):
    row = lax.broadcasted_iota(jnp.int32, a.shape, 0)
    return jnp.where(row >= 1, pltpu.roll(a, 1, 0), fill)


def running_sum(a):
    inside = lane_scan(a, jnp.add, 0.0)
    return inside + before(row_scan(last_lane(inside), jnp.add, 0.0), 0.0)


def running_max(a, seg):
    inside = lane_scan(a, jnp.maximum, LOW, seg)
    seg_end = last_lane(seg)
    ends = row_scan(last_lane(inside), jnp.maximum, LOW, seg_end)
    carried = jnp.where(before(seg_end, -1.0) == seg, before(ends, LOW), LOW)
    return jnp.maximum(inside, carried)


def column(cols, tile, size):
    per = size // 128
    return jnp.concatenate([cols[:, tile * per + i : tile * per + i + 1] for i in range(per)], 0)


def as_row(a, rows):
    return jnp.concatenate([a[i : i + 1, :] for i in range(rows)], 1)


def kernel(
    q_hbm, k_hbm, v_hbm, ig_ref, fg_ref, ds_ref, cmem_hbm, cnorm_ref, cmax_ref, w_hbm,
    out_ref,
    q_ref, k_ref, v_ref, cmem_ref,
    wfar, wown, stats, cpack, crecv, epack, erecv, num, den, hid, part_out, part_in, gates,
    in_sem, fsend, frecv, osend, orecv, oring, swap_send, ssend, srecv, srecv_rows,
    csend, crecv_sem, esend, erecv_sem, hsend, hrecv, psend, precv,
):
    me = lax.axis_index("seq")
    head = lax.axis_index("head")
    y, z = me // NZ, me % NZ
    x, core = head // 2, head % 2
    mate = 1 - core
    near = (x // 2) * 2 + (1 - x % 2)
    far = 3 - x
    home = (y // 2) == (x // 2)
    away = jnp.logical_not(home)
    opposite = ((y + 2) % NY) * NZ + z
    far_head = far * 2 + core

    def at(yy, zz):
        return ((yy + NY) % NY) * NZ + (zz + NZ) % NZ

    barrier = pltpu.get_barrier_semaphore()

    def greet(seq, hd):
        pl.semaphore_signal(
            barrier, inc=1, device_id={"seq": seq, "head": hd}, device_id_type=MESH
        )

    for d in range(1, NS):
        greet((me + d) % NS, head)
    greet(me, x * 2 + mate)
    greet(me, near * 2 + core)
    greet(me, far_head)

    @pl.when(away)
    def _():
        greet(opposite, far_head)

    loads = [
        pltpu.make_async_copy(a, b, in_sem.at[i])
        for i, (a, b) in enumerate(
            ((k_hbm, k_ref), (v_hbm, v_ref), (q_hbm, q_ref), (cmem_hbm, cmem_ref))
        )
    ]
    for load in loads:
        load.start()

    def remote(src, dst, send, recv, seq, hd):
        return pltpu.make_async_remote_copy(
            src_ref=src, dst_ref=dst, send_sem=send, recv_sem=recv,
            device_id={"seq": seq, "head": hd}, device_id_type=MESH,
        )

    def total(ref, count, sem):
        part = ref.at[pl.ds(0, count)]
        return pltpu.make_async_copy(part, part, sem)

    lf = fg_ref[...]
    lf = jnp.minimum(lf, 0.0) - jnp.log1p(jnp.exp(-jnp.abs(lf)))
    decay = running_sum(lf)
    seg = running_sum(ds_ref[...].astype(F32))
    u = ig_ref[...] - decay
    top = running_max(u, seg)
    local_max = decay + top
    end = lambda a: jnp.broadcast_to(a[7:8, 127:128], (1, 128))
    seg_end = end(seg)
    coeff = jnp.where(seg == seg_end, jnp.exp(jnp.minimum(u - end(top), 0.0)), 0.0) * (DK**-0.5)
    coeff_cols = jnp.transpose(coeff)
    top_cols = jnp.transpose(top)
    seg_cols = jnp.transpose(seg)

    loads[0].wait()
    keyed = [
        k_ref[i * 128 : (i + 1) * 128, :].astype(F32) * coeff_cols[:, i : i + 1] for i in range(8)
    ]
    normal = sum(jnp.sum(t, axis=0, keepdims=True) for t in keyed)
    stats[me, 0:1, :] = normal[:, :128]
    stats[me, 1:2, :] = normal[:, 128:]
    stats[me, 2:3, :] = end(local_max)
    stats[me, 3:4, :] = end(decay)
    stats[me, 4:5, :] = jnp.where(seg_end > 0.5, 1.0, 0.0)
    loads[1].wait()
    memory = lax.dot_general(
        jnp.concatenate([t.astype(BF16) for t in keyed], 0), v_ref[...],
        (((0,), (0,)), ((), ())), preferred_element_type=F32,
    ).astype(BF16)
    cpack[0:16] = memory[:, :256].reshape(16, 16, 256)
    cpack[16:32] = memory[:, 256:].reshape(16, 16, 256)
    crecv[me] = cpack[me]

    pl.semaphore_wait(barrier, jnp.where(home, 34, 35))

    mine_row = (y % 2) * NZ + z
    upper, lower = w_hbm.at[pl.ds(0, 64)], w_hbm.at[pl.ds(64, 64)]
    first, second = 2 * mine_row, 2 * mine_row + 1
    stay = pltpu.make_async_copy(upper, wown.at[first], in_sem.at[4])

    @pl.when(home)
    def _():
        stay.start()
        remote(lower, wown.at[second], swap_send, orecv.at[opposite], opposite, head).start()

    @pl.when(away)
    def _():
        remote(upper, wfar.at[first], swap_send, frecv.at[me], me, far_head).start()
        remote(lower, wfar.at[second], swap_send, frecv.at[opposite], opposite, far_head).start()

    for d in range(1, NS):
        dev = (me + d) % NS
        remote(cpack.at[dev], crecv.at[me], csend, crecv_sem, dev, head).start()
    for d in range(1, NZ):
        remote(stats.at[me], stats.at[me], ssend, srecv, at(y, z + d), head).start()

    def place(yy, zz):
        yy = (yy + NY) % NY
        half = jnp.where((yy // 2) == (x // 2), 0, 1)
        return ((yy % 2) * NZ + (zz + NZ) % NZ) * 2 + half

    def f_copy(yy, zz, dev):
        piece = wfar.at[place(yy, zz)]
        return remote(piece, piece, fsend, frecv.at[at(yy, zz)], dev, head)

    def o_copy(yy, dev):
        piece = wown.at[place(yy, z)]
        return remote(piece, piece, osend, orecv.at[at(yy, z)], dev, head)

    def r_copy(a, zz, dev):
        row = a * NZ + (zz + NZ) % NZ
        piece = wown.at[pl.ds(row * 2, 2)]
        return remote(piece, piece, osend, oring.at[row], dev, head)

    def f_sends(yy, zz, zs, ys):
        for dz in zs:
            f_copy(yy, zz, at(y, z + dz)).start()
        for dy in ys:
            f_copy(yy, zz, at(y + dy, z)).start()

    def z_step(k):
        f_copy(y, z - k, me).wait_recv()
        f_sends(y, z - k, (1,) if k <= 3 else (), (1, -1))
        if k <= 3:
            f_copy(y, z + k, me).wait_recv()
            f_sends(y, z + k, (-1,) if k <= 2 else (), (1, -1))

    def y_step(o, up):
        f_copy(y - 1, z + o, me).wait_recv()
        f_copy(y + 1, z + o, me).wait_recv()
        if up:
            f_sends(y - 1, z + o, (), (1,))
        else:
            f_sends(y + 1, z + o, (), (-1,))

    def attend(tile):
        n = (tile + 1) * QT
        qt = q_ref[tile * QT : (tile + 1) * QT, :]
        scores = lax.dot_general(
            qt, k_ref[:n, :], (((1,), (1,)), ((), ())), preferred_element_type=F32
        )
        blocks = n // 128
        u_row, seg_row = as_row(u, blocks), as_row(seg, blocks)
        spot = lax.broadcasted_iota(jnp.int32, (QT, n), 0) + tile * QT
        allowed = (lax.broadcasted_iota(jnp.int32, (QT, n), 1) <= spot) & (
            seg_row == column(seg_cols, tile, QT)
        )
        gain = jnp.exp(u_row - column(top_cols, tile, QT))
        weights = jnp.where(allowed, gain * (DK**-0.5), 0.0) * scores
        den[tile * QT : (tile + 1) * QT, :] = jnp.sum(weights, axis=1, keepdims=True)
        num[tile * QT : (tile + 1) * QT, :] = jnp.dot(
            weights.astype(BF16), v_ref[:n, :], preferred_element_type=F32
        )

    loads[2].wait()
    attend(0)
    f_copy(y, z, me).wait_recv()
    f_sends(y, z, (1, -1), (1, -1))
    attend(1)
    total(stats, NZ - 1, srecv).wait()
    row = stats.at[pl.ds(pl.multiple_of(y * NZ, NZ), NZ)]
    for dy in (1, 2, 3):
        remote(row, row, ssend, srecv_rows, at(y + dy, z), head).start()

    @pl.when(home)
    def _():
        stay.wait()
        remote(lower, wown.at[second], swap_send, orecv.at[opposite], opposite, head).wait_send()

    @pl.when(away)
    def _():
        pltpu.make_async_copy(w_hbm, w_hbm, swap_send).wait()
        o_copy(y, me).wait_recv()

    for dy in (1, -1):
        o_copy(y, at(y + dy, z)).start()
    attend(2)
    z_step(1)
    attend(3)

    loads[3].wait()
    total(stats, NS - NZ, srecv_rows).wait()
    m = jnp.broadcast_to(cmax_ref[...], (1, 128))
    n0, n1 = cnorm_ref[0:1, :], cnorm_ref[1:2, :]
    em, e0, e1 = m, n0, n1
    for j in range(NS - 1):
        keep = stats[j, 4:5, :] < 0.5
        inward = m + stats[j, 3:4, :]
        later = stats[j, 2:3, :]
        m = jnp.where(keep, jnp.maximum(inward, later), later)
        old = jnp.where(keep, jnp.exp(jnp.minimum(inward - m, 0.0)), 0.0)
        new = jnp.exp(later - m)
        n0 = old * n0 + new * stats[j, 0:1, :]
        n1 = old * n1 + new * stats[j, 1:2, :]
        here = me == j + 1
        em, e0, e1 = (jnp.where(here, b, a) for a, b in ((em, m), (e0, n0), (e1, n1)))
        gates[j, 0:1, :] = old
        gates[j, 1:2, :] = new

    inward = jnp.broadcast_to(em, (8, 128)) + decay
    fresh = seg < 0.5
    merged = jnp.where(fresh, jnp.maximum(inward, local_max), local_max)
    carried = jnp.where(fresh, jnp.exp(jnp.minimum(inward - merged, 0.0)), 0.0)
    own = jnp.exp(local_max - merged)
    carried_cols, own_cols = jnp.transpose(carried), jnp.transpose(own)
    en = jnp.concatenate([e0, e1], 1)
    high = en.astype(BF16)
    rest = en - high.astype(F32)
    mid = rest.astype(BF16)
    low = (rest - mid.astype(F32)).astype(BF16)
    norms = jnp.concatenate(
        [high.astype(F32), mid.astype(F32), low.astype(F32), jnp.zeros((5, DK), F32)], 0
    ).astype(BF16)
    sden = lax.dot_general(
        q_ref[...], norms, (((1,), (1,)), ((), ())), preferred_element_type=F32
    )
    sden = jnp.sum(sden, axis=1, keepdims=True)
    for i in range(8):
        rows = slice(i * 128, (i + 1) * 128)
        o, c = own_cols[:, i : i + 1], carried_cols[:, i : i + 1]
        whole = o * den[rows, :] + c * sden[rows, :]
        inverse = 1.0 / jnp.maximum(jnp.abs(whole), 1.0)
        den[rows, :] = c * inverse
        num[rows, :] = num[rows, :] * (o * inverse)
    z_step(2)

    group, half = me % 16, me // 16
    carry_rows = cmem_ref[pl.ds(pl.multiple_of(group * 16, 16), 16), :]
    state = jnp.where(half == 0, carry_rows[:, :256], carry_rows[:, 256:])
    total(crecv, NS - 1, crecv_sem).wait()
    epack[0] = state.astype(BF16)
    for j in range(NS - 1):
        old = jnp.concatenate([gates[j, 0:1, :]] * 2, 1)
        new = jnp.concatenate([gates[j, 1:2, :]] * 2, 1)
        state = old * state + new * crecv[j].astype(F32)
        epack[j + 1] = state.astype(BF16)
    erecv[me] = epack[me]
    for d in range(1, NS):
        dev = (me + d) % NS
        remote(epack.at[dev], erecv.at[me], esend, erecv_sem, dev, head).start()

    z_step(3)
    z_step(4)
    o_copy(y - 1, me).wait_recv()
    o_copy(y + 1, me).wait_recv()
    lift = z % 2 == 0
    o_copy(jnp.where(lift, y + 3, y + 1), at(jnp.where(lift, y + 1, y + 3), z)).start()
    order = (
        (0, True), (-1, True), (1, False), (-2, False),
        (2, True), (-3, True), (3, False), (-4, False),
    )
    for o, up in order:
        y_step(o, up)

    total(erecv, NS - 1, erecv_sem).wait()
    entry_a = erecv[0:16].reshape(256, 256)
    entry_b = erecv[16:32].reshape(256, 256)
    mine, theirs = (x % 2) * 2 + core, (x % 2) * 2 + mate
    other, other_mate = (1 - x % 2) * 2 + core, (1 - x % 2) * 2 + mate

    def rows_of(t):
        return pl.ds(pl.multiple_of(t * XT, XT), XT)

    def h_copy(slot, t, hd):
        tile = hid.at[slot, rows_of(t)]
        return remote(tile, tile, hsend, hrecv.at[slot, t], me, hd)

    def make_hidden(t, c):
        rows = rows_of(t)
        qt = q_ref[rows, :]
        scale = den[rows, :]
        for part, e in ((slice(0, 256), entry_a), (slice(256, 512), entry_b)):
            got = jnp.dot(qt, e, preferred_element_type=F32)
            hid[mine, rows, part] = (num[rows, part] + scale * got).astype(BF16)
        h_copy(mine, t, near * 2 + core).start()
        h_copy(mine, t, x * 2 + mate).start()
        return c

    lax.fori_loop(0, NXT, make_hidden, 0)

    o_copy(y + 2, me).wait_recv()
    for a in (0, 1):
        for dz in (1, -1):
            r_copy(a, z, at(y, z + dz)).start()
    for o, _ in order:
        f_copy(y + 2, z + o, me).wait_recv()

    def p_copy(t):
        return remote(
            part_out.at[rows_of(t)], part_in.at[rows_of(t)], psend, precv.at[t], me, far_head
        )

    def project(t, w_ref):
        whole = None
        for j in range(4):
            w = w_ref[8 * j : 8 * j + 8].reshape(DV, DV)
            term = jnp.dot(hid[j, rows_of(t), :], w, preferred_element_type=F32)
            whole = term if whole is None else whole + term
        return whole

    def ring_step(t):
        k, a = t // 2 + 1, t % 2

        @pl.when(k <= 4 - a)
        def _():
            r_copy(a, z - k, me).wait_recv()

        @pl.when(k <= 3 - a)
        def _():
            r_copy(a, z - k, at(y, z + 1)).start()

        @pl.when(k <= 3 + a)
        def _():
            r_copy(a, z + k, me).wait_recv()

        @pl.when(k <= 2 + a)
        def _():
            r_copy(a, z + k, at(y, z - 1)).start()

    def cross(t, c):
        h_copy(other, t, head).wait_recv()
        h_copy(other, t, x * 2 + mate).start()
        h_copy(theirs, t, head).wait_recv()
        h_copy(other_mate, t, head).wait_recv()
        part_out[rows_of(t), :] = project(t, wfar).astype(BF16)
        p_copy(t).start()
        ring_step(t)
        return c

    lax.fori_loop(0, NXT, cross, 0)

    def finish(t, c):
        kept = project(t, wown)
        p_copy(t).wait_recv()
        rows = rows_of(t)
        out_ref[rows, :] = (kept + part_in[rows, :].astype(F32)).astype(BF16)
        return c

    lax.fori_loop(0, NXT, finish, 0)

    total(wfar, 31, fsend).wait()
    total(wown, 31, osend).wait()
    total(stats, 31, ssend).wait()
    total(cpack, 31, csend).wait()
    total(epack, 31, esend).wait()
    total(hid, 3, hsend).wait()
    pltpu.make_async_copy(part_out, part_out, psend).wait()


def shards(q, k, v, ig, fg, ds, cmem, cnorm, cmax, w):
    dma = pltpu.SemaphoreType.DMA
    vmem = pl.BlockSpec(memory_space=pltpu.VMEM)
    hbm = pl.BlockSpec(memory_space=pl.ANY)
    return pl.pallas_call(
        kernel,
        out_shape=jax.ShapeDtypeStruct((TOK, DV), BF16),
        in_specs=[hbm, hbm, hbm, vmem, vmem, vmem, hbm, vmem, vmem, hbm],
        out_specs=vmem,
        scratch_shapes=[
            pltpu.VMEM((TOK, DK), BF16),
            pltpu.VMEM((TOK, DK), BF16),
            pltpu.VMEM((TOK, DV), BF16),
            pltpu.VMEM((DK, DV), F32),
            pltpu.VMEM((NS, 64, DV), BF16),
            pltpu.VMEM((NS, 64, DV), BF16),
            pltpu.VMEM((NS, 8, 128), F32),
            pltpu.VMEM((NS, 16, 256), BF16),
            pltpu.VMEM((NS, 16, 256), BF16),
            pltpu.VMEM((NS, 16, 256), BF16),
            pltpu.VMEM((NS, 16, 256), BF16),
            pltpu.VMEM((TOK, DV), F32),
            pltpu.VMEM((TOK, 1), F32),
            pltpu.VMEM((4, TOK, DV), BF16),
            pltpu.VMEM((TOK, DV), BF16),
            pltpu.VMEM((TOK, DV), BF16),
            pltpu.VMEM((NS, 8, 128), F32),
            dma((5,)), dma, dma((NS,)), dma, dma((NS,)), dma((16,)), dma, dma, dma, dma,
            dma, dma, dma, dma, dma, dma((4, NXT)), dma, dma((NXT,)),
        ],
        compiler_params=pltpu.CompilerParams(
            collective_id=0, has_side_effects=True, vmem_limit_bytes=56 * 2**20
        ),
    )(
        q, k, v, ig.reshape(8, 128), fg.reshape(8, 128), ds.reshape(8, 128),
        cmem.reshape(DK, DV), cnorm.reshape(2, 128), cmax.reshape(1, 1), w,
    )


def solution(mesh):
    placed = (
        P("seq", "head"),
        P("seq", "head"),
        P("seq", "head"),
        P("head", "seq"),
        P("head", "seq"),
        P("seq"),
        P("head", None, None),
        P("head", None),
        P("head"),
        P("seq", "head"),
    )
    return jax.shard_map(
        shards, mesh=mesh, in_specs=placed, out_specs=P("seq", "head"), check_vma=False
    )
```

time: 91.7 us -> 77.3 us (0.84)
  Pallas kernels: 88.6 us -> 74.2 us
    pallas_call x1, Pallas kernels: 88.6 us -> 74.2 us  [shards(): pl.pallas_call(kernel, out_shape=jax.ShapeDtypeStruct((TOK, DV), BF16), i...]
where the time goes in v2:
time: 77.3 us; the launch traced here: 77.1 us
  Pallas kernels  74.2 us (96%)
  local copies, waits for them, and re-layouts  2.26 us (3%)
    pallas_call x1, Pallas kernels, shards(): pl.pallas_call(kernel, out_shape=jax.ShapeDtypeStruct((TOK, DV), BF16), i...  74.2 us
    unnamed x1, local copies, waits for them, and re-layouts  2.26 us

profile of v2, /device:TPU:1, one launch (start us, length us, event | category | flops | bytes accessed | tf_op | source)
XLA Modules:
  0.0 77.1 jit_solution(6072737979860772824)
XLA Ops:
  0.7 74.2 %shard_map.100 = bf16[1024,512]{1,0:T(8,128)(2,1)} custom-call(bf16[1024,256]{1,0:T(8,128)(2,1)} %q_hbm.1, bf16[1024,256]{1,0:T(8,128)(2,1)} %k_hbm.1, bf16[1024,512]{1,0:T(8,128)(2,1)} %v_hbm.1, f32[8,128]{1,0:T(8,128)} %bitcast.8, f32[8,128]{1,0:T(8,128)} %bitcast.9, s32[8,128]{1,0:T(8,128)} %bitcast.10, f32[256,512]{1,0:T(8,128)} %bitcast.7, ...), custom_call_target="tpu_custom_call" | custom-call | tf_op jit(solution)/shard_map/pallas_call | solution.py:444
  74.9 2.3 %copy.13 = bf16[1024,512]{1,0:T(8,128)(2,1)} copy(bf16[1024,512]{1,0:T(8,128)(2,1)} %shard_map.100) | data formatting | bytes 2097152

commit v3 on v2

--- a/solution.py
+++ b/solution.py
@@ -70,11 +70,11 @@
 
 
 def kernel(
-    q_hbm, k_hbm, v_hbm, ig_ref, fg_ref, ds_ref, cmem_hbm, cnorm_ref, cmax_ref, w_hbm,
-    out_ref,
-    q_ref, k_ref, v_ref, cmem_ref,
+    q_hbm, k_hbm, v_hbm, ig_hbm, fg_hbm, ds_hbm, cmem_hbm, cnorm_hbm, cmax_hbm, w_hbm,
+    out_hbm,
+    q_ref, k_ref, v_ref, cmem_ref, ig_ref, fg_ref, ds_ref, cnorm_ref, cmax_ref, out_ref,
     wfar, wown, stats, cpack, crecv, epack, erecv, num, den, hid, part_out, part_in, gates,
-    in_sem, fsend, frecv, osend, orecv, oring, swap_send, ssend, srecv, srecv_rows,
+    in_sem, out_sem, row_sem, fsend, frecv, osend, orecv, oring, swap_send, ssend, srecv, srecv_rows,
     csend, crecv_sem, esend, erecv_sem, hsend, hrecv, psend, precv,
 ):
     me = lax.axis_index("seq")
@@ -99,8 +99,10 @@
             barrier, inc=1, device_id={"seq": seq, "head": hd}, device_id_type=MESH
         )
 
-    for d in range(1, NS):
-        greet((me + d) % NS, head)
+    for d in range(1, NZ):
+        greet(at(y, z + d), head)
+    for d in range(1, NY):
+        greet(at(y + d, z), head)
     greet(me, x * 2 + mate)
     greet(me, near * 2 + core)
     greet(me, far_head)
@@ -112,7 +114,11 @@
     loads = [
         pltpu.make_async_copy(a, b, in_sem.at[i])
         for i, (a, b) in enumerate(
-            ((k_hbm, k_ref), (v_hbm, v_ref), (q_hbm, q_ref), (cmem_hbm, cmem_ref))
+            (
+                (fg_hbm, fg_ref), (ds_hbm, ds_ref), (ig_hbm, ig_ref), (k_hbm, k_ref),
+                (v_hbm, v_ref), (q_hbm, q_ref), (cmem_hbm, cmem_ref), (cnorm_hbm, cnorm_ref),
+                (cmax_hbm, cmax_ref),
+            )
         )
     ]
     for load in loads:
@@ -128,6 +134,8 @@
         part = ref.at[pl.ds(0, count)]
         return pltpu.make_async_copy(part, part, sem)
 
+    for i in range(3):
+        loads[i].wait()
     lf = fg_ref[...]
     lf = jnp.minimum(lf, 0.0) - jnp.log1p(jnp.exp(-jnp.abs(lf)))
     decay = running_sum(lf)
@@ -142,7 +150,7 @@
     top_cols = jnp.transpose(top)
     seg_cols = jnp.transpose(seg)
 
-    loads[0].wait()
+    loads[3].wait()
     keyed = [
         k_ref[i * 128 : (i + 1) * 128, :].astype(F32) * coeff_cols[:, i : i + 1] for i in range(8)
     ]
@@ -152,7 +160,32 @@
     stats[me, 2:3, :] = end(local_max)
     stats[me, 3:4, :] = end(decay)
     stats[me, 4:5, :] = jnp.where(seg_end > 0.5, 1.0, 0.0)
-    loads[1].wait()
+    pl.semaphore_wait(barrier, jnp.where(home, 13, 14))
+
+    mine_row = (y % 2) * NZ + z
+    upper, lower = w_hbm.at[pl.ds(0, 64)], w_hbm.at[pl.ds(64, 64)]
+    first, second = 2 * mine_row, 2 * mine_row + 1
+    stay = pltpu.make_async_copy(upper, wown.at[first], in_sem.at[9])
+
+    @pl.when(home)
+    def _():
+        stay.start()
+        remote(lower, wown.at[second], swap_send, orecv.at[opposite], opposite, head).start()
+
+    @pl.when(away)
+    def _():
+        remote(upper, wfar.at[first], swap_send, frecv.at[me], me, far_head).start()
+        remote(lower, wfar.at[second], swap_send, frecv.at[opposite], opposite, far_head).start()
+
+    for d in range(1, NZ):
+        remote(stats.at[me], stats.at[me], ssend, srecv, at(y, z + d), head).start()
+
+    for d in range(1, NY):
+        pl.semaphore_signal(
+            row_sem, inc=1, device_id={"seq": at(y + d, z), "head": head}, device_id_type=MESH
+        )
+
+    loads[4].wait()
     memory = lax.dot_general(
         jnp.concatenate([t.astype(BF16) for t in keyed], 0), v_ref[...],
         (((0,), (0,)), ((), ())), preferred_element_type=F32,
@@ -161,29 +194,6 @@
     cpack[16:32] = memory[:, 256:].reshape(16, 16, 256)
     crecv[me] = cpack[me]
 
-    pl.semaphore_wait(barrier, jnp.where(home, 34, 35))
-
-    mine_row = (y % 2) * NZ + z
-    upper, lower = w_hbm.at[pl.ds(0, 64)], w_hbm.at[pl.ds(64, 64)]
-    first, second = 2 * mine_row, 2 * mine_row + 1
-    stay = pltpu.make_async_copy(upper, wown.at[first], in_sem.at[4])
-
-    @pl.when(home)
-    def _():
-        stay.start()
-        remote(lower, wown.at[second], swap_send, orecv.at[opposite], opposite, head).start()
-
-    @pl.when(away)
-    def _():
-        remote(upper, wfar.at[first], swap_send, frecv.at[me], me, far_head).start()
-        remote(lower, wfar.at[second], swap_send, frecv.at[opposite], opposite, far_head).start()
-
-    for d in range(1, NS):
-        dev = (me + d) % NS
-        remote(cpack.at[dev], crecv.at[me], csend, crecv_sem, dev, head).start()
-    for d in range(1, NZ):
-        remote(stats.at[me], stats.at[me], ssend, srecv, at(y, z + d), head).start()
-
     def place(yy, zz):
         yy = (yy + NY) % NY
         half = jnp.where((yy // 2) == (x // 2), 0, 1)
@@ -242,11 +252,14 @@
             weights.astype(BF16), v_ref[:n, :], preferred_element_type=F32
         )
 
-    loads[2].wait()
-    attend(0)
     f_copy(y, z, me).wait_recv()
     f_sends(y, z, (1, -1), (1, -1))
-    attend(1)
+    pl.semaphore_wait(row_sem, NY - 1)
+    for d in range(1, NS):
+        dev = (me + d) % NS
+        remote(cpack.at[dev], crecv.at[me], csend, crecv_sem, dev, head).start()
+    loads[5].wait()
+    attend(0)
     total(stats, NZ - 1, srecv).wait()
     row = stats.at[pl.ds(pl.multiple_of(y * NZ, NZ), NZ)]
     for dy in (1, 2, 3):
@@ -264,11 +277,14 @@
 
     for dy in (1, -1):
         o_copy(y, at(y + dy, z)).start()
+    z_step(1)
+    attend(1)
     attend(2)
-    z_step(1)
+    z_step(2)
     attend(3)
 
-    loads[3].wait()
+    for i in (6, 7, 8):
+        loads[i].wait()
     total(stats, NS - NZ, srecv_rows).wait()
     m = jnp.broadcast_to(cmax_ref[...], (1, 128))
     n0, n1 = cnorm_ref[0:1, :], cnorm_ref[1:2, :]
@@ -312,7 +328,7 @@
         inverse = 1.0 / jnp.maximum(jnp.abs(whole), 1.0)
         den[rows, :] = c * inverse
         num[rows, :] = num[rows, :] * (o * inverse)
-    z_step(2)
+    z_step(3)
 
     group, half = me % 16, me // 16
     carry_rows = cmem_ref[pl.ds(pl.multiple_of(group * 16, 16), 16), :]
@@ -329,7 +345,6 @@
         dev = (me + d) % NS
         remote(epack.at[dev], erecv.at[me], esend, erecv_sem, dev, head).start()
 
-    z_step(3)
     z_step(4)
     o_copy(y - 1, me).wait_recv()
     o_copy(y + 1, me).wait_recv()
@@ -424,6 +439,7 @@
         p_copy(t).wait_recv()
         rows = rows_of(t)
         out_ref[rows, :] = (kept + part_in[rows, :].astype(F32)).astype(BF16)
+        pltpu.make_async_copy(out_ref.at[rows], out_hbm.at[rows], out_sem).start()
         return c
 
     lax.fori_loop(0, NXT, finish, 0)
@@ -435,22 +451,39 @@
     total(epack, 31, esend).wait()
     total(hid, 3, hsend).wait()
     pltpu.make_async_copy(part_out, part_out, psend).wait()
+    pltpu.make_async_copy(out_ref, out_hbm, out_sem).wait()
+
+
+def hand_on(src, dst, sem):
+    parts = [
+        pltpu.make_async_copy(src.at[pl.ds(i * 128, 128)], dst.at[pl.ds(i * 128, 128)], sem.at[i])
+        for i in range(TOK // 128)
+    ]
+    for part in parts:
+        part.start()
+    for part in parts:
+        part.wait()
 
 
 def shards(q, k, v, ig, fg, ds, cmem, cnorm, cmax, w):
     dma = pltpu.SemaphoreType.DMA
-    vmem = pl.BlockSpec(memory_space=pltpu.VMEM)
     hbm = pl.BlockSpec(memory_space=pl.ANY)
-    return pl.pallas_call(
+    mixed = pl.pallas_call(
         kernel,
         out_shape=jax.ShapeDtypeStruct((TOK, DV), BF16),
-        in_specs=[hbm, hbm, hbm, vmem, vmem, vmem, hbm, vmem, vmem, hbm],
-        out_specs=vmem,
+        in_specs=[hbm] * 10,
+        out_specs=hbm,
         scratch_shapes=[
             pltpu.VMEM((TOK, DK), BF16),
             pltpu.VMEM((TOK, DK), BF16),
             pltpu.VMEM((TOK, DV), BF16),
             pltpu.VMEM((DK, DV), F32),
+            pltpu.VMEM((8, 128), F32),
+            pltpu.VMEM((8, 128), F32),
+            pltpu.VMEM((8, 128), jnp.int32),
+            pltpu.VMEM((2, 128), F32),
+            pltpu.VMEM((1, 1), F32),
+            pltpu.VMEM((TOK, DV), BF16),
             pltpu.VMEM((NS, 64, DV), BF16),
             pltpu.VMEM((NS, 64, DV), BF16),
             pltpu.VMEM((NS, 8, 128), F32),
@@ -464,7 +497,7 @@
             pltpu.VMEM((TOK, DV), BF16),
             pltpu.VMEM((TOK, DV), BF16),
             pltpu.VMEM((NS, 8, 128), F32),
-            dma((5,)), dma, dma((NS,)), dma, dma((NS,)), dma((16,)), dma, dma, dma, dma,
+            dma((10,)), dma, pltpu.SemaphoreType.REGULAR, dma, dma((NS,)), dma, dma((NS,)), dma((16,)), dma, dma, dma, dma,
             dma, dma, dma, dma, dma, dma((4, NXT)), dma, dma((NXT,)),
         ],
         compiler_params=pltpu.CompilerParams(
@@ -474,6 +507,14 @@
         q, k, v, ig.reshape(8, 128), fg.reshape(8, 128), ds.reshape(8, 128),
         cmem.reshape(DK, DV), cnorm.reshape(2, 128), cmax.reshape(1, 1), w,
     )
+    return pl.pallas_call(
+        hand_on,
+        out_shape=jax.ShapeDtypeStruct((TOK, DV), BF16),
+        in_specs=[hbm],
+        out_specs=hbm,
+        scratch_shapes=[dma((TOK // 128,))],
+        compiler_params=pltpu.CompilerParams(vmem_limit_bytes=56 * 2**20),
+    )(mixed)
 
 
 def solution(mesh):

time: 77.3 us -> 106 us (1.37)
  Pallas kernels: 74.2 us -> 106 us
  local copies, waits for them, and re-layouts: 2.26 us -> 0 us
    pallas_call x0 -> x1, Pallas kernels: none -> 32.9 us  [shards(): pl.pallas_call(hand_on, out_shape=jax.ShapeDtypeStruct((TOK, DV), BF16),...]
    unnamed x1 -> x0, local copies, waits for them, and re-layouts: 2.26 us -> none
    pallas_call x1, Pallas kernels: 74.2 us -> 72.6 us  [shards(): pl.pallas_call(kernel, out_shape=jax.ShapeDtypeStruct((TOK, DV), BF16), i...]
where the time goes in v3:
time: 106 us
  Pallas kernels  106 us (100%)
    pallas_call x1, Pallas kernels, shards(): pl.pallas_call(kernel, out_shape=jax.ShapeDtypeStruct((TOK, DV), BF16), i...  72.6 us
    pallas_call x1, Pallas kernels, shards(): pl.pallas_call(hand_on, out_shape=jax.ShapeDtypeStruct((TOK, DV), BF16),...  32.9 us

profile of v3, /device:TPU:1, one launch (start us, length us, event | category | flops | bytes accessed | tf_op | source)
XLA Modules:
  0.0 106.2 jit_solution(79170569678020621)
XLA Ops:
  0.7 72.6 %shard_map.100.src = bf16[1024,512]{1,0:T(8,128)(2,1)} custom-call(bf16[1024,256]{1,0:T(8,128)(2,1)} %q_hbm.1, bf16[1024,256]{1,0:T(8,128)(2,1)} %k_hbm.1, bf16[1024,512]{1,0:T(8,128)(2,1)} %v_hbm.1, f32[8,128]{1,0:T(8,128)} %bitcast.8, f32[8,128]{1,0:T(8,128)} %bitcast.9, s32[8,128]{1,0:T(8,128)} %bitcast.10, f32[256,512]{1,0:T(8,128)} %bitcast.7, ...), custom_call_target="tpu_custom_call" | custom-call | tf_op jit(solution)/shard_map/pallas_call | solution.py:471
  73.3 32.9 %shard_map.101 = bf16[1024,512]{1,0:T(8,128)(2,1)} custom-call(bf16[1024,512]{1,0:T(8,128)(2,1)} %shard_map.100.src), custom_call_target="tpu_custom_call" | custom-call | tf_op jit(solution)/shard_map/pallas_call | solution.py:510

commit v4 on v3

--- a/solution.py
+++ b/solution.py
@@ -71,11 +71,11 @@
 
 def kernel(
     q_hbm, k_hbm, v_hbm, ig_hbm, fg_hbm, ds_hbm, cmem_hbm, cnorm_hbm, cmax_hbm, w_hbm,
-    out_hbm,
-    q_ref, k_ref, v_ref, cmem_ref, ig_ref, fg_ref, ds_ref, cnorm_ref, cmax_ref, out_ref,
-    wfar, wown, stats, cpack, crecv, epack, erecv, num, den, hid, part_out, part_in, gates,
-    in_sem, out_sem, row_sem, fsend, frecv, osend, orecv, oring, swap_send, ssend, srecv, srecv_rows,
-    csend, crecv_sem, esend, erecv_sem, hsend, hrecv, psend, precv,
+    out_ref,
+    q_ref, k_ref, v_ref, cmem_ref, ig_ref, fg_ref, ds_ref, cnorm_ref, cmax_ref,
+    wfar, wown, stats, rowstats, cpack, crecv, tpack, trecv, epack, erecv, num, den, hid, part_out, part_in, gates,
+    in_sem, fsend, frecv, osend, orecv, oring, swap_send, ssend, srecv, srecv_rows,
+    csend, crecv_sem, tsend, trecv_sem, esend, erecv_sem, hsend, hrecv, psend, precv,
 ):
     me = lax.axis_index("seq")
     head = lax.axis_index("head")
@@ -180,19 +180,16 @@
     for d in range(1, NZ):
         remote(stats.at[me], stats.at[me], ssend, srecv, at(y, z + d), head).start()
 
-    for d in range(1, NY):
-        pl.semaphore_signal(
-            row_sem, inc=1, device_id={"seq": at(y + d, z), "head": head}, device_id_type=MESH
-        )
-
     loads[4].wait()
     memory = lax.dot_general(
         jnp.concatenate([t.astype(BF16) for t in keyed], 0), v_ref[...],
         (((0,), (0,)), ((), ())), preferred_element_type=F32,
     ).astype(BF16)
-    cpack[0:16] = memory[:, :256].reshape(16, 16, 256)
-    cpack[16:32] = memory[:, 256:].reshape(16, 16, 256)
-    crecv[me] = cpack[me]
+    cpack[...] = memory.reshape(NZ, DK // NZ, DV)
+    crecv[z] = cpack[z]
+    for d in range(1, NZ):
+        to = (z + d) % NZ
+        remote(cpack.at[to], crecv.at[z], csend, crecv_sem, at(y, to), head).start()
 
     def place(yy, zz):
         yy = (yy + NY) % NY
@@ -254,16 +251,31 @@
 
     f_copy(y, z, me).wait_recv()
     f_sends(y, z, (1, -1), (1, -1))
-    pl.semaphore_wait(row_sem, NY - 1)
-    for d in range(1, NS):
-        dev = (me + d) % NS
-        remote(cpack.at[dev], crecv.at[me], csend, crecv_sem, dev, head).start()
     loads[5].wait()
     attend(0)
     total(stats, NZ - 1, srecv).wait()
-    row = stats.at[pl.ds(pl.multiple_of(y * NZ, NZ), NZ)]
+    base = y * NZ
+    m = jnp.full((1, 128), LOW, F32)
+    g = r = n0 = n1 = jnp.zeros((1, 128), F32)
+    prefixes = []
+    for k in range(NZ):
+        prefixes.append((m, g, r, n0, n1))
+        m2, g2, r2 = (stats[base + k, c : c + 1, :] for c in (2, 3, 4))
+        inward = m + g2
+        m = jnp.where(r2 < 0.5, jnp.maximum(inward, m2), m2)
+        old = jnp.where(r2 < 0.5, jnp.exp(jnp.minimum(inward - m, 0.0)), 0.0)
+        new = jnp.exp(m2 - m)
+        n0 = old * n0 + new * stats[base + k, 0:1, :]
+        n1 = old * n1 + new * stats[base + k, 1:2, :]
+        g, r = g + g2, jnp.maximum(r, r2)
+        gates[k, 0:1, :] = old
+        gates[k, 1:2, :] = new
+    for c, value in enumerate((n0, n1, m, g, r)):
+        rowstats[y, c : c + 1, :] = value
     for dy in (1, 2, 3):
-        remote(row, row, ssend, srecv_rows, at(y + dy, z), head).start()
+        remote(
+            rowstats.at[y], rowstats.at[y], ssend, srecv_rows, at(y + dy, z), head
+        ).start()
 
     @pl.when(home)
     def _():
@@ -279,29 +291,41 @@
         o_copy(y, at(y + dy, z)).start()
     z_step(1)
     attend(1)
+    y_step(0, True)
     attend(2)
     z_step(2)
     attend(3)
 
     for i in (6, 7, 8):
         loads[i].wait()
-    total(stats, NS - NZ, srecv_rows).wait()
+    total(rowstats, NY - 1, srecv_rows).wait()
     m = jnp.broadcast_to(cmax_ref[...], (1, 128))
     n0, n1 = cnorm_ref[0:1, :], cnorm_ref[1:2, :]
+    for row_at in range(NY - 1):
+        m2, g2, r2 = (rowstats[row_at, c : c + 1, :] for c in (2, 3, 4))
+        inward = m + g2
+        after = jnp.where(r2 < 0.5, jnp.maximum(inward, m2), m2)
+        old = jnp.where(r2 < 0.5, jnp.exp(jnp.minimum(inward - after, 0.0)), 0.0)
+        new = jnp.exp(m2 - after)
+        earlier = row_at < y
+        n0 = jnp.where(earlier, old * n0 + new * rowstats[row_at, 0:1, :], n0)
+        n1 = jnp.where(earlier, old * n1 + new * rowstats[row_at, 1:2, :], n1)
+        m = jnp.where(earlier, after, m)
+        gates[NZ + row_at, 0:1, :] = old
+        gates[NZ + row_at, 1:2, :] = new
     em, e0, e1 = m, n0, n1
-    for j in range(NS - 1):
-        keep = stats[j, 4:5, :] < 0.5
-        inward = m + stats[j, 3:4, :]
-        later = stats[j, 2:3, :]
-        m = jnp.where(keep, jnp.maximum(inward, later), later)
-        old = jnp.where(keep, jnp.exp(jnp.minimum(inward - m, 0.0)), 0.0)
-        new = jnp.exp(later - m)
-        n0 = old * n0 + new * stats[j, 0:1, :]
-        n1 = old * n1 + new * stats[j, 1:2, :]
-        here = me == j + 1
-        em, e0, e1 = (jnp.where(here, b, a) for a, b in ((em, m), (e0, n0), (e1, n1)))
-        gates[j, 0:1, :] = old
-        gates[j, 1:2, :] = new
+    for k in range(NZ):
+        m2, g2, r2, p0, p1 = prefixes[k]
+        inward = m + g2
+        after = jnp.where(r2 < 0.5, jnp.maximum(inward, m2), m2)
+        old = jnp.where(r2 < 0.5, jnp.exp(jnp.minimum(inward - after, 0.0)), 0.0)
+        new = jnp.exp(m2 - after)
+        here = z == k
+        em = jnp.where(here, after, em)
+        e0 = jnp.where(here, old * n0 + new * p0, e0)
+        e1 = jnp.where(here, old * n1 + new * p1, e1)
+        gates[NZ + NY + k, 0:1, :] = old
+        gates[NZ + NY + k, 1:2, :] = new
 
     inward = jnp.broadcast_to(em, (8, 128)) + decay
     fresh = seg < 0.5
@@ -328,38 +352,46 @@
         inverse = 1.0 / jnp.maximum(jnp.abs(whole), 1.0)
         den[rows, :] = c * inverse
         num[rows, :] = num[rows, :] * (o * inverse)
+
+    def factor(j, kind):
+        return jnp.concatenate([gates[j, kind : kind + 1, :]] * (DV // 128), 1)
+
+    total(crecv, NZ - 1, crecv_sem).wait()
+    part = jnp.zeros((DK // NZ, DV), F32)
+    parts = []
+    for k in range(NZ):
+        parts.append(part)
+        part = factor(k, 0) * part + factor(k, 1) * crecv[k].astype(F32)
+    tpack[...] = part.astype(BF16)
+    for dy in (1, 2, 3):
+        remote(tpack, trecv.at[y], tsend, trecv_sem, at(y + dy, z), head).start()
     z_step(3)
-
-    group, half = me % 16, me // 16
-    carry_rows = cmem_ref[pl.ds(pl.multiple_of(group * 16, 16), 16), :]
-    state = jnp.where(half == 0, carry_rows[:, :256], carry_rows[:, 256:])
-    total(crecv, NS - 1, crecv_sem).wait()
-    epack[0] = state.astype(BF16)
-    for j in range(NS - 1):
-        old = jnp.concatenate([gates[j, 0:1, :]] * 2, 1)
-        new = jnp.concatenate([gates[j, 1:2, :]] * 2, 1)
-        state = old * state + new * crecv[j].astype(F32)
-        epack[j + 1] = state.astype(BF16)
-    erecv[me] = epack[me]
-    for d in range(1, NS):
-        dev = (me + d) % NS
-        remote(epack.at[dev], erecv.at[me], esend, erecv_sem, dev, head).start()
+    y_step(-1, True)
+    y_step(1, False)
+
+    state = cmem_ref[pl.ds(pl.multiple_of(z * (DK // NZ), DK // NZ), DK // NZ), :]
+    total(trecv, NY - 1, trecv_sem).wait()
+    for row_at in range(NY - 1):
+        joined = factor(NZ + row_at, 0) * state + factor(NZ + row_at, 1) * trecv[row_at].astype(F32)
+        state = jnp.where(row_at < y, joined, state)
+    for k in range(NZ):
+        at_k = NZ + NY + k
+        epack[k] = (factor(at_k, 0) * state + factor(at_k, 1) * parts[k]).astype(BF16)
+    erecv[z] = epack[z]
+    for d in range(1, NZ):
+        to = (z + d) % NZ
+        remote(epack.at[to], erecv.at[z], esend, erecv_sem, at(y, to), head).start()
 
     z_step(4)
     o_copy(y - 1, me).wait_recv()
     o_copy(y + 1, me).wait_recv()
     lift = z % 2 == 0
     o_copy(jnp.where(lift, y + 3, y + 1), at(jnp.where(lift, y + 1, y + 3), z)).start()
-    order = (
-        (0, True), (-1, True), (1, False), (-2, False),
-        (2, True), (-3, True), (3, False), (-4, False),
-    )
-    for o, up in order:
-        y_step(o, up)
-
-    total(erecv, NS - 1, erecv_sem).wait()
-    entry_a = erecv[0:16].reshape(256, 256)
-    entry_b = erecv[16:32].reshape(256, 256)
+
+    y_step(-2, False)
+    y_step(2, True)
+    total(erecv, NZ - 1, erecv_sem).wait()
+    entry = erecv[...].reshape(DK, DV)
     mine, theirs = (x % 2) * 2 + core, (x % 2) * 2 + mate
     other, other_mate = (1 - x % 2) * 2 + core, (1 - x % 2) * 2 + mate
 
@@ -374,20 +406,22 @@
         rows = rows_of(t)
         qt = q_ref[rows, :]
         scale = den[rows, :]
-        for part, e in ((slice(0, 256), entry_a), (slice(256, 512), entry_b)):
-            got = jnp.dot(qt, e, preferred_element_type=F32)
-            hid[mine, rows, part] = (num[rows, part] + scale * got).astype(BF16)
+        got = jnp.dot(qt, entry, preferred_element_type=F32)
+        hid[mine, rows, :] = (num[rows, :] + scale * got).astype(BF16)
         h_copy(mine, t, near * 2 + core).start()
         h_copy(mine, t, x * 2 + mate).start()
         return c
 
     lax.fori_loop(0, NXT, make_hidden, 0)
 
+    y_step(-3, True)
+    y_step(3, False)
+    y_step(-4, False)
     o_copy(y + 2, me).wait_recv()
     for a in (0, 1):
         for dz in (1, -1):
             r_copy(a, z, at(y, z + dz)).start()
-    for o, _ in order:
+    for o in range(-4, 4):
         f_copy(y + 2, z + o, me).wait_recv()
 
     def p_copy(t):
@@ -439,40 +473,28 @@
         p_copy(t).wait_recv()
         rows = rows_of(t)
         out_ref[rows, :] = (kept + part_in[rows, :].astype(F32)).astype(BF16)
-        pltpu.make_async_copy(out_ref.at[rows], out_hbm.at[rows], out_sem).start()
         return c
 
     lax.fori_loop(0, NXT, finish, 0)
 
     total(wfar, 31, fsend).wait()
     total(wown, 31, osend).wait()
-    total(stats, 31, ssend).wait()
-    total(cpack, 31, csend).wait()
-    total(epack, 31, esend).wait()
+    total(stats, NZ - 1 + NY - 1, ssend).wait()
+    total(cpack, NZ - 1, csend).wait()
+    total(trecv, NY - 1, tsend).wait()
+    total(epack, NZ - 1, esend).wait()
     total(hid, 3, hsend).wait()
     pltpu.make_async_copy(part_out, part_out, psend).wait()
-    pltpu.make_async_copy(out_ref, out_hbm, out_sem).wait()
-
-
-def hand_on(src, dst, sem):
-    parts = [
-        pltpu.make_async_copy(src.at[pl.ds(i * 128, 128)], dst.at[pl.ds(i * 128, 128)], sem.at[i])
-        for i in range(TOK // 128)
-    ]
-    for part in parts:
-        part.start()
-    for part in parts:
-        part.wait()
 
 
 def shards(q, k, v, ig, fg, ds, cmem, cnorm, cmax, w):
     dma = pltpu.SemaphoreType.DMA
     hbm = pl.BlockSpec(memory_space=pl.ANY)
-    mixed = pl.pallas_call(
+    return pl.pallas_call(
         kernel,
-        out_shape=jax.ShapeDtypeStruct((TOK, DV), BF16),
+        out_shape=pltpu.VMEM((TOK, DV), BF16),
         in_specs=[hbm] * 10,
-        out_specs=hbm,
+        out_specs=pl.BlockSpec(memory_space=pltpu.VMEM),
         scratch_shapes=[
             pltpu.VMEM((TOK, DK), BF16),
             pltpu.VMEM((TOK, DK), BF16),
@@ -483,38 +505,32 @@
             pltpu.VMEM((8, 128), jnp.int32),
             pltpu.VMEM((2, 128), F32),
             pltpu.VMEM((1, 1), F32),
-            pltpu.VMEM((TOK, DV), BF16),
             pltpu.VMEM((NS, 64, DV), BF16),
             pltpu.VMEM((NS, 64, DV), BF16),
             pltpu.VMEM((NS, 8, 128), F32),
-            pltpu.VMEM((NS, 16, 256), BF16),
-            pltpu.VMEM((NS, 16, 256), BF16),
-            pltpu.VMEM((NS, 16, 256), BF16),
-            pltpu.VMEM((NS, 16, 256), BF16),
+            pltpu.VMEM((NY, 8, 128), F32),
+            pltpu.VMEM((NZ, DK // NZ, DV), BF16),
+            pltpu.VMEM((NZ, DK // NZ, DV), BF16),
+            pltpu.VMEM((DK // NZ, DV), BF16),
+            pltpu.VMEM((NY, DK // NZ, DV), BF16),
+            pltpu.VMEM((NZ, DK // NZ, DV), BF16),
+            pltpu.VMEM((NZ, DK // NZ, DV), BF16),
             pltpu.VMEM((TOK, DV), F32),
             pltpu.VMEM((TOK, 1), F32),
             pltpu.VMEM((4, TOK, DV), BF16),
             pltpu.VMEM((TOK, DV), BF16),
             pltpu.VMEM((TOK, DV), BF16),
             pltpu.VMEM((NS, 8, 128), F32),
-            dma((10,)), dma, pltpu.SemaphoreType.REGULAR, dma, dma((NS,)), dma, dma((NS,)), dma((16,)), dma, dma, dma, dma,
-            dma, dma, dma, dma, dma, dma((4, NXT)), dma, dma((NXT,)),
+            dma((10,)), dma, dma((NS,)), dma, dma((NS,)), dma((16,)), dma, dma, dma, dma,
+            dma, dma, dma, dma, dma, dma, dma, dma((4, NXT)), dma, dma((NXT,)),
         ],
         compiler_params=pltpu.CompilerParams(
-            collective_id=0, has_side_effects=True, vmem_limit_bytes=56 * 2**20
+            collective_id=0, has_side_effects=True, vmem_limit_bytes=60 * 2**20
         ),
     )(
         q, k, v, ig.reshape(8, 128), fg.reshape(8, 128), ds.reshape(8, 128),
         cmem.reshape(DK, DV), cnorm.reshape(2, 128), cmax.reshape(1, 1), w,
     )
-    return pl.pallas_call(
-        hand_on,
-        out_shape=jax.ShapeDtypeStruct((TOK, DV), BF16),
-        in_specs=[hbm],
-        out_specs=hbm,
-        scratch_shapes=[dma((TOK // 128,))],
-        compiler_params=pltpu.CompilerParams(vmem_limit_bytes=56 * 2**20),
-    )(mixed)
 
 
 def solution(mesh):

time: 106 us -> 73.3 us (0.69)
  Pallas kernels: 106 us -> 71.6 us
    pallas_call x2 -> x1, Pallas kernels: 106 us -> 71.6 us  [shards(): pl.pallas_call(kernel, out_shape=pltpu.VMEM((TOK, DV), BF16), in_specs=[h...]
where the time goes in v4:
time: 73.3 us; the launch traced here: 73.2 us
  Pallas kernels  71.6 us (98%)
  local copies, waits for them, and re-layouts  0.97 us (1%)
    pallas_call x1, Pallas kernels, shards(): pl.pallas_call(kernel, out_shape=pltpu.VMEM((TOK, DV), BF16), in_specs=[h...  71.6 us

profile of v4, /device:TPU:1, one launch (start us, length us, event | category | flops | bytes accessed | tf_op | source)
XLA Modules:
  0.0 73.2 jit_solution(6213065227311431021)
XLA Ops:
  0.7 71.6 %shard_map.100 = bf16[1024,512]{1,0:T(8,128)(2,1)S(1)} custom-call(bf16[1024,256]{1,0:T(8,128)(2,1)} %q_hbm.1, bf16[1024,256]{1,0:T(8,128)(2,1)} %k_hbm.1, bf16[1024,512]{1,0:T(8,128)(2,1)} %v_hbm.1, f32[8,128]{1,0:T(8,128)} %bitcast.8, f32[8,128]{1,0:T(8,128)} %bitcast.9, s32[8,128]{1,0:T(8,128)} %bitcast.10, f32[256,512]{1,0:T(8,128)} %bitcast.7, ...), custom_call_target="tpu_custom_call" | custom-call | tf_op jit(solution)/shard_map/pallas_call | solution.py:493
  72.3 1.0 %copy.12 = bf16[1024,512]{1,0:T(8,128)(2,1)} copy(bf16[1024,512]{1,0:T(8,128)(2,1)S(1)} %shard_map.100) | data formatting | bytes 2097152

commit v5 on v4

--- a/solution.py
+++ b/solution.py
@@ -215,12 +215,12 @@
         for dy in ys:
             f_copy(yy, zz, at(y + dy, z)).start()
 
-    def z_step(k):
+    def z_step(k, ys=(1, -1)):
         f_copy(y, z - k, me).wait_recv()
-        f_sends(y, z - k, (1,) if k <= 3 else (), (1, -1))
+        f_sends(y, z - k, (1,) if k <= 3 else (), ys)
         if k <= 3:
             f_copy(y, z + k, me).wait_recv()
-            f_sends(y, z + k, (-1,) if k <= 2 else (), (1, -1))
+            f_sends(y, z + k, (-1,) if k <= 2 else (), ys)
 
     def y_step(o, up):
         f_copy(y - 1, z + o, me).wait_recv()
@@ -293,7 +293,7 @@
     attend(1)
     y_step(0, True)
     attend(2)
-    z_step(2)
+    z_step(2, ())
     attend(3)
 
     for i in (6, 7, 8):
@@ -365,9 +365,9 @@
     tpack[...] = part.astype(BF16)
     for dy in (1, 2, 3):
         remote(tpack, trecv.at[y], tsend, trecv_sem, at(y + dy, z), head).start()
-    z_step(3)
-    y_step(-1, True)
-    y_step(1, False)
+    z_step(3, ())
+    for k in (2, -2):
+        f_sends(y, z - k, (), (1, -1))
 
     state = cmem_ref[pl.ds(pl.multiple_of(z * (DK // NZ), DK // NZ), DK // NZ), :]
     total(trecv, NY - 1, trecv_sem).wait()
@@ -382,12 +382,16 @@
         to = (z + d) % NZ
         remote(epack.at[to], erecv.at[z], esend, erecv_sem, at(y, to), head).start()
 
+    for k in (3, -3):
+        f_sends(y, z - k, (), (1, -1))
     z_step(4)
     o_copy(y - 1, me).wait_recv()
     o_copy(y + 1, me).wait_recv()
     lift = z % 2 == 0
     o_copy(jnp.where(lift, y + 3, y + 1), at(jnp.where(lift, y + 1, y + 3), z)).start()
 
+    y_step(-1, True)
+    y_step(1, False)
     y_step(-2, False)
     y_step(2, True)
     total(erecv, NZ - 1, erecv_sem).wait()

time: 73.3 us -> 71.9 us (0.981)
  Pallas kernels: 71.6 us -> 70.2 us
    pallas_call x1, Pallas kernels: 71.6 us -> 70.2 us  [shards(): pl.pallas_call(kernel, out_shape=pltpu.VMEM((TOK, DV), BF16), in_specs=[h...]
where the time goes in v5:
time: 71.9 us
  Pallas kernels  70.2 us (98%)
  local copies, waits for them, and re-layouts  0.97 us (1%)
    pallas_call x1, Pallas kernels, shards(): pl.pallas_call(kernel, out_shape=pltpu.VMEM((TOK, DV), BF16), in_specs=[h...  70.2 us

profile of v5, /device:TPU:1, one launch (start us, length us, event | category | flops | bytes accessed | tf_op | source)
XLA Modules:
  0.0 71.9 jit_solution(15390112248386386131)
XLA Ops:
  0.7 70.2 %shard_map.100 = bf16[1024,512]{1,0:T(8,128)(2,1)S(1)} custom-call(bf16[1024,256]{1,0:T(8,128)(2,1)} %q_hbm.1, bf16[1024,256]{1,0:T(8,128)(2,1)} %k_hbm.1, bf16[1024,512]{1,0:T(8,128)(2,1)} %v_hbm.1, f32[8,128]{1,0:T(8,128)} %bitcast.8, f32[8,128]{1,0:T(8,128)} %bitcast.9, s32[8,128]{1,0:T(8,128)} %bitcast.10, f32[256,512]{1,0:T(8,128)} %bitcast.7, ...), custom_call_target="tpu_custom_call" | custom-call | tf_op jit(solution)/shard_map/pallas_call | solution.py:497
  70.9 1.0 %copy.12 = bf16[1024,512]{1,0:T(8,128)(2,1)} copy(bf16[1024,512]{1,0:T(8,128)(2,1)S(1)} %shard_map.100) | data formatting | bytes 2097152

commit v6 on v5

--- a/solution.py
+++ b/solution.py
@@ -86,7 +86,7 @@
     far = 3 - x
     home = (y // 2) == (x // 2)
     away = jnp.logical_not(home)
-    opposite = ((y + 2) % NY) * NZ + z
+    opposite = (NY - 1 - y) * NZ + z
     far_head = far * 2 + core
 
     def at(yy, zz):
@@ -194,7 +194,7 @@
     def place(yy, zz):
         yy = (yy + NY) % NY
         half = jnp.where((yy // 2) == (x // 2), 0, 1)
-        return ((yy % 2) * NZ + (zz + NZ) % NZ) * 2 + half
+        return (((yy + half) % 2) * NZ + (zz + NZ) % NZ) * 2 + half
 
     def f_copy(yy, zz, dev):
         piece = wfar.at[place(yy, zz)]
@@ -384,14 +384,14 @@
 
     for k in (3, -3):
         f_sends(y, z - k, (), (1, -1))
+    y_step(-1, True)
+    y_step(1, False)
     z_step(4)
     o_copy(y - 1, me).wait_recv()
     o_copy(y + 1, me).wait_recv()
     lift = z % 2 == 0
     o_copy(jnp.where(lift, y + 3, y + 1), at(jnp.where(lift, y + 1, y + 3), z)).start()
 
-    y_step(-1, True)
-    y_step(1, False)
     y_step(-2, False)
     y_step(2, True)
     total(erecv, NZ - 1, erecv_sem).wait()

time: 71.9 us -> 72.1 us (level)
  no operation moved by 1% of the time
where the time goes in v6:
time: 72.1 us; the launch traced here: 72 us
  Pallas kernels  70.3 us (98%)
  local copies, waits for them, and re-layouts  0.97 us (1%)
    pallas_call x1, Pallas kernels, shards(): pl.pallas_call(kernel, out_shape=pltpu.VMEM((TOK, DV), BF16), in_specs=[h...  70.3 us

profile of v6, /device:TPU:1, one launch (start us, length us, event | category | flops | bytes accessed | tf_op | source)
XLA Modules:
  0.0 72.0 jit_solution(12745145028559443743)
XLA Ops:
  0.7 70.3 %shard_map.100 = bf16[1024,512]{1,0:T(8,128)(2,1)S(1)} custom-call(bf16[1024,256]{1,0:T(8,128)(2,1)} %q_hbm.1, bf16[1024,256]{1,0:T(8,128)(2,1)} %k_hbm.1, bf16[1024,512]{1,0:T(8,128)(2,1)} %v_hbm.1, f32[8,128]{1,0:T(8,128)} %bitcast.8, f32[8,128]{1,0:T(8,128)} %bitcast.9, s32[8,128]{1,0:T(8,128)} %bitcast.10, f32[256,512]{1,0:T(8,128)} %bitcast.7, ...), custom_call_target="tpu_custom_call" | custom-call | tf_op jit(solution)/shard_map/pallas_call | solution.py:497
  71.0 1.0 %copy.12 = bf16[1024,512]{1,0:T(8,128)(2,1)} copy(bf16[1024,512]{1,0:T(8,128)(2,1)S(1)} %shard_map.100) | data formatting | bytes 2097152
